TPU v7x, 256 devices: a whole 4x4x8 slice. The times are simulated.
256 devices in a mesh: dp: 16 (over z_lo, y, core), expert: 16 (over x, z_hi).
Axes of the slice: x: 4, y: 4, z: 8 (z_hi: 4, z_lo: 2; z = z_hi * 2 + z_lo), core: 2. Of those that a mesh axis runs over, the one named last changes fastest.
Arguments:
- tokens: bfloat16 [32768, 2048], P(('dp', 'expert')), may hold values from -6 to 6
- cotangent: bfloat16 [32768, 2048], P(('dp', 'expert')), may hold values from -24 to 24
- expert_ids: int32 [32768, 4], P(('dp', 'expert')), may hold values from 0 to 15, all different within a row; in each aligned block of 128 rows (0 to 127, 128 to 255, ...) at most 34 rows name the same one
- gate_codes: int32 [32768, 4], P(('dp', 'expert')), may hold values from 1 to 16
- gate_weight: bfloat16 [16, 2048, 768], P('expert'), may hold values from -0.125 to 0.125
- up_weight: bfloat16 [16, 2048, 768], P('expert'), may hold values from -0.125 to 0.125
- down_weight: bfloat16 [16, 768, 2048], P('expert'), may hold values from -0.21875 to 0.21875
Outputs:
- grad_tokens: bfloat16 [32768, 2048], P(('dp', 'expert'))
- grad_gate: float32 [16, 2048, 768], P('expert', 'dp')
- grad_up: float32 [16, 2048, 768], P('expert', 'dp')
- grad_down: float32 [16, 768, 2048], P('expert', None, 'dp')
Inputs may be any that keep to these rules, and one draw needn't show every extreme that they name: `expert_ids`: within the 128 rows of one device each row names 4 different experts and no expert is named by more than 34 rows; in some devices' rows an expert is named by exactly 34 rows.
All inputs are finite; a program needn't handle non-finite values.
Results may differ from a plain program's by a relative error of at most 0.0063.
Values may be sent and summed in bfloat16 or wider, within the bound.
A program may use at most 128 MiB of HBM per device.

v0:
```python
import jax
import jax.numpy as jnp
from jax import lax
from jax.sharding import PartitionSpec as P

TOP = 4


def dispatch_tables(expert_ids, gate_codes, experts, capacity):
    tok_rows, top_count = expert_ids.shape
    flat_ids = expert_ids.reshape(-1)
    columns = jnp.arange(experts, dtype=jnp.int32)
    expert_hits = (flat_ids[:, None] == columns[None, :]).astype(jnp.int32)
    before = jnp.cumsum(expert_hits, axis=0) - expert_hits
    slot_ranks = jnp.sum(before * expert_hits, axis=1)
    target = flat_ids * capacity + slot_ranks
    slot_ids = jnp.arange(experts * capacity, dtype=jnp.int32)
    matched = (slot_ids[:, None] == target[None, :]).reshape(
        experts * capacity, tok_rows, top_count
    )
    placer = jnp.sum(matched.astype(jnp.float32), axis=2).astype(jnp.bfloat16)
    scales = gate_codes.astype(jnp.float32) / 16.0
    weighted = jnp.sum(jnp.where(matched, scales[None, :, :], 0.0), axis=2).astype(jnp.bfloat16)
    return (placer, weighted)


def front_rows(x_rows, u_rows, gate_weight, up_weight, down_weight):
    gate_pre = jnp.einsum("slcd,ldh->slch", x_rows, gate_weight, preferred_element_type=jnp.float32)
    up_pre = jnp.einsum("slcd,ldh->slch", x_rows, up_weight, preferred_element_type=jnp.float32)
    sigmoid_gate = jax.nn.sigmoid(gate_pre)
    active = gate_pre * sigmoid_gate
    hidden = (active * up_pre).astype(jnp.bfloat16)
    d_hidden = jnp.einsum("slcd,lhd->slch", u_rows, down_weight, preferred_element_type=jnp.float32)
    return (gate_pre, up_pre, sigmoid_gate, active, hidden, d_hidden)


def back_rows(front_terms, gate_weight, up_weight):
    gate_pre, up_pre, sigmoid_gate, active, hidden, d_hidden = front_terms
    d_gate = (d_hidden * up_pre * sigmoid_gate * (1.0 + gate_pre * (1.0 - sigmoid_gate))).astype(
        jnp.bfloat16
    )
    d_up = (d_hidden * active).astype(jnp.bfloat16)
    row_grads = (
        jnp.einsum("slch,ldh->slcd", d_gate, gate_weight, preferred_element_type=jnp.float32)
        + jnp.einsum("slch,ldh->slcd", d_up, up_weight, preferred_element_type=jnp.float32)
    ).astype(jnp.bfloat16)
    return (d_gate, d_up, row_grads)


def down_terms(u_rows, hidden):
    return jnp.einsum("slcd,slch->dlh", u_rows, hidden, preferred_element_type=jnp.float32)


def on_device(tokens, cotangent, expert_ids, gate_codes, gate_weight, up_weight, down_weight):
    expert_ranks = lax.axis_size("expert")
    local_count, features, hidden_size = gate_weight.shape
    experts = expert_ranks * local_count
    tok_rows = tokens.shape[0]
    capacity = tok_rows * TOP * 17 // (experts * 16)
    placer, weighted = dispatch_tables(expert_ids, gate_codes, experts, capacity)
    send_shape = (expert_ranks, local_count, capacity, features)
    send_tokens = (
        jnp.dot(placer, tokens, preferred_element_type=jnp.float32)
        .astype(jnp.bfloat16)
        .reshape(send_shape)
    )
    send_cotangent = (
        jnp.dot(weighted, cotangent, preferred_element_type=jnp.float32)
        .astype(jnp.bfloat16)
        .reshape(send_shape)
    )
    x_rows = lax.all_to_all(send_tokens, "expert", split_axis=0, concat_axis=0, tiled=True)
    u_rows = lax.all_to_all(send_cotangent, "expert", split_axis=0, concat_axis=0, tiled=True)
    front_terms = front_rows(x_rows, u_rows, gate_weight, up_weight, down_weight)
    hidden = front_terms[4]
    d_gate, d_up, row_grads = back_rows(front_terms, gate_weight, up_weight)
    returned = lax.all_to_all(row_grads, "expert", split_axis=0, concat_axis=0, tiled=True)
    returned_flat = returned.reshape(experts * capacity, features)
    grad_tokens = lax.dot_general(
        placer, returned_flat, (((0,), (0,)), ((), ())), preferred_element_type=jnp.float32
    ).astype(jnp.bfloat16)
    gate_part = jnp.einsum("slcd,slch->dlh", x_rows, d_gate, preferred_element_type=jnp.float32)
    up_part = jnp.einsum("slcd,slch->dlh", x_rows, d_up, preferred_element_type=jnp.float32)
    all_sums = lax.psum_scatter(
        jnp.concatenate(
            [jnp.concatenate([gate_part, up_part], axis=2), down_terms(u_rows, hidden)], axis=2
        ),
        "dp",
        scatter_dimension=0,
        tiled=True,
    )
    gate_up_part = all_sums[:, :, : 2 * hidden_size]
    down_part = all_sums[:, :, 2 * hidden_size :]
    grad_gate = jnp.transpose(gate_up_part[:, :, :hidden_size], (1, 0, 2))
    grad_up = jnp.transpose(gate_up_part[:, :, hidden_size:], (1, 0, 2))
    grad_down = jnp.transpose(down_part, (1, 2, 0))
    return (grad_tokens, grad_gate, grad_up, grad_down)


def solution(mesh):
    in_specs = (
        P(("dp", "expert"), None),
        P(("dp", "expert"), None),
        P(("dp", "expert"), None),
        P(("dp", "expert"), None),
        P("expert", None, None),
        P("expert", None, None),
        P("expert", None, None),
    )
    out_specs = (
        P(("dp", "expert"), None),
        P("expert", "dp", None),
        P("expert", "dp", None),
        P("expert", None, "dp"),
    )
    return jax.shard_map(
        on_device, mesh=mesh, in_specs=in_specs, out_specs=out_specs, check_vma=False
    )
```

profile of v0, /device:TPU:1, one launch (start us, length us, event | category | flops | bytes accessed | tf_op | source)
XLA Modules:
  0.0 361.1 jit_solution(16828675460579070651)
XLA Ops:
  9.0 1.2 reduce-window.6
  11.7 3.2 convolution_convert_fusion
  14.8 4.2 %reshape.99 = bf16[16,1,34,2048]{3,2,0,1:T(8,128)(2,1)} reshape(bf16[544,2048]{1,0:T(8,128)(2,1)} %convolution_convert_fusion) | data formatting | bytes 4456448 | tf_op jit(solution)/shard_map/reshape | solution.py:65
  19.0 11.6 %all-to-all-start.1 = ((bf16[16,1,34,2048]{3,2,1,0:T(8,128)(2,1)}), bf16[16,1,34,2048]{3,2,1,0:T(8,128)(2,1)}, u32[]{:S(2)}, u32[]{:S(2)}) async-start(bf16[16,1,34,2048]{3,2,1,0:T(8,128)(2,1)} %bitcast.161), calls=%async_computation.1 | async-start | bytes 5242880 | tf_op jit(solution)/shard_map/all_to_all | solution.py:72
  30.6 3.2 convolution_convert_fusion.1
  33.8 4.2 %reshape.96 = bf16[16,1,34,2048]{3,2,0,1:T(8,128)(2,1)} reshape(bf16[544,2048]{1,0:T(8,128)(2,1)} %convolution_convert_fusion.1) | data formatting | bytes 4456448 | tf_op jit(solution)/shard_map/reshape | solution.py:70
  38.0 49.9 %all-to-all-done.1 = bf16[16,1,34,2048]{3,2,1,0:T(8,128)(2,1)} async-done(((bf16[16,1,34,2048]{3,2,1,0:T(8,128)(2,1)}), bf16[16,1,34,2048]{3,2,1,0:T(8,128)(2,1)}, u32[]{:S(2)}, u32[]{:S(2)}) %all-to-all-start.1) | async-done | bytes 2228256 | tf_op jit(solution)/shard_map/all_to_all | solution.py:72
  87.9 9.3 %all-to-all-start = ((bf16[16,1,34,2048]{3,2,1,0:T(8,128)(2,1)}), bf16[16,1,34,2048]{3,2,1,0:T(8,128)(2,1)}, u32[]{:S(2)}, u32[]{:S(2)}) async-start(bf16[16,1,34,2048]{3,2,1,0:T(8,128)(2,1)} %bitcast.160), calls=%async_computation | async-start | bytes 5242880 | tf_op jit(solution)/shard_map/all_to_all | solution.py:73
  97.4 5.5 %fusion.2 = f32[16,34,768]{2,1,0:T(8,128)} fusion(bf16[1,2048,768]{2,1,0:T(8,128)(2,1)S(1)} %copy-done, bf16[16,1,34,2048]{3,2,1,0:T(8,128)(2,1)} %all-to-all-done.1), kind=kOutput, calls=%fused_computation.7 | convolution fusion | flops 1711276032 | bytes 7045120 | tf_op jit(solution)/shard_map/slcd,ldh->slch/dot_general | solution.py:28
  102.8 5.3 %fusion.5 = f32[16,34,768]{2,1,0:T(8,128)} fusion(bf16[1,2048,768]{2,1,0:T(8,128)(2,1)S(1)} %copy-done.5, bf16[16,1,34,2048]{3,2,1,0:T(8,128)(2,1)} %all-to-all-done.1), kind=kOutput, calls=%fused_computation.10 | convolution fusion | flops 1711276032 | bytes 7045120 | tf_op jit(solution)/shard_map/slcd,ldh->slch/dot_general | solution.py:29
  108.1 38.4 %all-to-all-done = bf16[16,1,34,2048]{3,2,1,0:T(8,128)(2,1)} async-done(((bf16[16,1,34,2048]{3,2,1,0:T(8,128)(2,1)}), bf16[16,1,34,2048]{3,2,1,0:T(8,128)(2,1)}, u32[]{:S(2)}, u32[]{:S(2)}) %all-to-all-start) | async-done | bytes 2228256 | tf_op jit(solution)/shard_map/all_to_all | solution.py:73
  146.5 5.8 %convolution_bitcast_fusion = f32[2048,1,768]{0,2,1:T(8,128)S(1)} fusion(bf16[16,1,34,2048]{3,2,1,0:T(8,128)(2,1)} %all-to-all-done, f32[16,34,768]{2,1,0:T(8,128)} %fusion.5, f32[16,34,768]{2,1,0:T(8,128)} %fusion.2), kind=kOutput, calls=%fused_computation.2 | convolution fusion | flops 1713782784 | bytes 11862016 | tf_op jit(solution)/shard_map/slcd,slch->dlh/dot_general | solution.py:51
  152.4 4.6 %fusion.27 = (bf16[16,34,768]{2,1,0:T(8,128)(2,1)S(1)}, bf16[16,1,34,768]{3,2,0,1:T(8,128)(2,1)S(1)}) fusion(f32[16,34,768]{2,1,0:T(8,128)S(1)} %copy-done.7, f32[16,34,768]{2,1,0:T(8,128)S(1)} %copy-done.8, bf16[1,768,2048]{2,1,0:T(8,128)(2,1)S(1)} %copy-done.4, bf16[16,1,34,2048]{3,2,1,0:T(8,128)(2,1)} %all-to-all-done), kind=kOutput, calls=%fused_computation.42 | convolution fusion | flops 1716707328 | bytes 10387456 | tf_op jit(solution)/shard_map/slcd,lhd->slch/dot_general | solution.py:33
  156.9 5.1 %convolution_bitcast_fusion.1 = f32[2048,1,768]{0,2,1:T(8,128)S(1)} fusion(bf16[16,34,768]{2,1,0:T(8,128)(2,1)S(1)} %get-tuple-element.26, bf16[16,1,34,2048]{3,2,1,0:T(8,128)(2,1)} %all-to-all-done.1), kind=kOutput, calls=%fused_computation.3 | convolution fusion | flops 1711276032 | bytes 9355264 | tf_op jit(solution)/shard_map/slcd,slch->dlh/dot_general | solution.py:83
  162.1 4.7 %convolution_bitcast_fusion.2 = f32[2048,1,768]{0,2,1:T(8,128)S(1)} fusion(bf16[16,1,34,2048]{3,2,1,0:T(8,128)(2,1)} %all-to-all-done.1, bf16[16,1,34,768]{3,2,0,1:T(8,128)(2,1)S(1)} %get-tuple-element.27), kind=kOutput, calls=%fused_computation.4 | convolution fusion | flops 1711276032 | bytes 9355264 | tf_op jit(solution)/shard_map/slcd,slch->dlh/dot_general | solution.py:82
  166.8 7.0 %pad_maximum_fusion = f32[2048,1,2304]{0,2,1:T(8,128)} fusion(f32[2048,1,768]{0,2,1:T(8,128)S(1)} %convolution_bitcast_fusion, f32[2048,1,768]{0,2,1:T(8,128)S(1)} %convolution_bitcast_fusion.1, f32[2048,1,768]{0,2,1:T(8,128)S(1)} %convolution_bitcast_fusion.2), kind=kLoop, calls=%fused_computation | loop fusion | flops 9437184 | bytes 37748736 | tf_op jit(solution)/shard_map/concatenate | solution.py:85
  173.8 3.6 fusion
  177.4 2.3 fusion.9
  179.7 93.2 %all_to_all.15 = bf16[16,1,34,2048]{3,2,1,0:T(8,128)(2,1)} all-to-all(bf16[16,1,34,2048]{3,2,1,0:T(8,128)(2,1)S(1)} %fusion.9), channel_id=1, replica_groups=mesh['dp'=16,'expert'=16] {'expert'}, dimensions={0} | all-to-all | bytes 4456448 | tf_op jit(solution)/shard_map/all_to_all | solution.py:77
  272.9 4.2 %reshape.105 = bf16[544,2048]{1,0:T(8,128)(2,1)} reshape(bf16[16,1,34,2048]{3,2,1,0:T(8,128)(2,1)} %all_to_all.15) | data formatting | bytes 4456448 | tf_op jit(solution)/shard_map/reshape | solution.py:78
  277.1 3.1 convolution_convert_fusion.2
  280.2 69.1 %reduce-scatter.2.cloned.1.call-done = f32[128,1,2304]{0,2,1:T(8,128)} async-done(((f32[2048,1,2304]{0,2,1:T(8,128)}), f32[128,1,2304]{0,2,1:T(8,128)}) %reduce-scatter.2.cloned.1.call-update) | async-done | bytes 1179664 | tf_op jit(solution)/shard_map/reduce_scatter | solution.py:84
  349.3 2.2 slice_bitcast_fusion
  351.5 1.9 copy.53
  (34 shorter events, 4.5 us)
Async XLA Ops:
  7.2 90.2 %copy-start = (bf16[1,2048,768]{2,1,0:T(8,128)(2,1)S(1)}, bf16[1,2048,768]{2,1,0:T(8,128)(2,1)}, u32[]{:S(2)}) copy-start(bf16[1,2048,768]{2,1,0:T(8,128)(2,1)} %param.11) | copy-start | bytes 9437188
  19.0 68.9 %all-to-all-start.1 = ((bf16[16,1,34,2048]{3,2,1,0:T(8,128)(2,1)}), bf16[16,1,34,2048]{3,2,1,0:T(8,128)(2,1)}, u32[]{:S(2)}, u32[]{:S(2)}) async-start(bf16[16,1,34,2048]{3,2,1,0:T(8,128)(2,1)} %bitcast.161), calls=%async_computation.1 | async-start | bytes 5242880 | tf_op jit(solution)/shard_map/all_to_all | solution.py:72
  87.9 58.7 %all-to-all-start = ((bf16[16,1,34,2048]{3,2,1,0:T(8,128)(2,1)}), bf16[16,1,34,2048]{3,2,1,0:T(8,128)(2,1)}, u32[]{:S(2)}, u32[]{:S(2)}) async-start(bf16[16,1,34,2048]{3,2,1,0:T(8,128)(2,1)} %bitcast.160), calls=%async_computation | async-start | bytes 5242880 | tf_op jit(solution)/shard_map/all_to_all | solution.py:73
  97.1 252.2 %reduce-scatter.2.cloned.1.call-start = ((), (), s32[]{:S(2)}) async-start(), calls=%async_computation.4 | async-start | bytes 20054016 | tf_op jit(solution)/shard_map/reduce_scatter | solution.py:84
  97.4 5.5 %copy-start.5 = (bf16[1,2048,768]{2,1,0:T(8,128)(2,1)S(1)}, bf16[1,2048,768]{2,1,0:T(8,128)(2,1)}, u32[]{:S(2)}) copy-start(bf16[1,2048,768]{2,1,0:T(8,128)(2,1)} %param.12) | copy-start | bytes 9437188
  146.5 5.8 %copy-start.4 = (bf16[1,768,2048]{2,1,0:T(8,128)(2,1)S(1)}, bf16[1,768,2048]{2,1,0:T(8,128)(2,1)}, u32[]{:S(2)}) copy-start(bf16[1,768,2048]{2,1,0:T(8,128)(2,1)} %param.13) | copy-start | bytes 9437188
  146.5 5.8 %copy-start.7 = (f32[16,34,768]{2,1,0:T(8,128)S(1)}, f32[16,34,768]{2,1,0:T(8,128)}, u32[]{:S(2)}) copy-start(f32[16,34,768]{2,1,0:T(8,128)} %fusion.2) | copy-start | bytes 5013508
  146.5 5.8 %copy-start.8 = (f32[16,34,768]{2,1,0:T(8,128)S(1)}, f32[16,34,768]{2,1,0:T(8,128)}, u32[]{:S(2)}) copy-start(f32[16,34,768]{2,1,0:T(8,128)} %fusion.5) | copy-start | bytes 5013508
  156.9 5.2 %copy-start.1 = (bf16[16,34,768]{2,1,0:T(8,128)(2,1)}, bf16[16,34,768]{2,1,0:T(8,128)(2,1)S(1)}, u32[]{:S(2)}) copy-start(bf16[16,34,768]{2,1,0:T(8,128)(2,1)S(1)} %get-tuple-element.26) | copy-start | bytes 2506756
  156.9 5.2 %copy-start.3 = (bf16[16,1,34,768]{3,2,0,1:T(8,128)(2,1)}, bf16[16,1,34,768]{3,2,0,1:T(8,128)(2,1)S(1)}, u32[]{:S(2)}) copy-start(bf16[16,1,34,768]{3,2,0,1:T(8,128)(2,1)S(1)} %get-tuple-element.27) | copy-start | bytes 2506756
  173.8 3.6 %copy-start.2 = (bf16[16,34,768]{2,1,0:T(8,128)(2,1)S(1)}, bf16[16,34,768]{2,1,0:T(8,128)(2,1)}, u32[]{:S(2)}) copy-start(bf16[16,34,768]{2,1,0:T(8,128)(2,1)} %copy-done.1) | copy-start | bytes 2506756
  173.8 3.6 %copy-start.6 = (bf16[1,2048,768]{2,1,0:T(8,128)(2,1)S(1)}, bf16[1,2048,768]{2,1,0:T(8,128)(2,1)}, u32[]{:S(2)}) copy-start(bf16[1,2048,768]{2,1,0:T(8,128)(2,1)} %param.12) | copy-start | bytes 9437188
Sparse Core Ops, SparseCore 0:
  173.9 175.3 reduce-scatter.1
where the time goes:
time: 365 us; the launch traced here: 361 us
  waiting for transfers between devices  157 us (43%)
  blocking collectives  93.2 us (26%)
  matrix products  46.2 us (13%)
  starting transfers between devices  21.1 us (6%)
  local copies, waits for them, and re-layouts  19.1 us (5%)
  between operations  14.2 us (4%)
  other arithmetic  9.91 us (3%)
    all_to_all x1, blocking collectives, on_device(): lax.all_to_all(row_grads, 'expert', split_axis=0, concat_axis=0, tiled=True)  93.2 us
    reduce_scatter x1, waiting for transfers between devices, on_device(): lax.psum_scatter(jnp.concatenate([jnp.concatenate([gate_part, up_part], a...  69.1 us
    all_to_all x1, waiting for transfers between devices, on_device(): lax.all_to_all(send_tokens, 'expert', split_axis=0, concat_axis=0, tiled=...  49.9 us
    all_to_all x1, waiting for transfers between devices, on_device(): lax.all_to_all(send_cotangent, 'expert', split_axis=0, concat_axis=0, til...  38.4 us
    all_to_all x1, starting transfers between devices, on_device(): lax.all_to_all(send_tokens, 'expert', split_axis=0, concat_axis=0, tiled=...  11.6 us
    all_to_all x1, starting transfers between devices, on_device(): lax.all_to_all(send_cotangent, 'expert', split_axis=0, concat_axis=0, til...  9.27 us
  transfers between devices with their start and end apart: 3, of which 3 were waited for; matrix products, arithmetic and copies ran while one was open for 9% of the time, Pallas kernels for 0%

commit v1 on v0

v1 whole, which is shorter than its diff:
```python
import functools

import jax
import jax.numpy as jnp
from jax import lax
from jax.experimental import pallas as pl
from jax.experimental.pallas import tpu as pltpu
from jax.sharding import PartitionSpec as P

TOP = 4
MESH = pl.DeviceIdType.MESH
F32 = jnp.float32
BF16 = jnp.bfloat16
NX, NZ, NY, NZL, NC = 4, 4, 4, 2, 2
NT = (((1,), (1,)), ((), ()))


def up16(n):
    return -(-n // 16) * 16


def kernel(
    cap, tok, cot, gcode, wg_any, wu_any, wd_any,
    gt_out, gg_out, gu_out, gd_out,
    wg, wu, wd, gz, zt, zc, slots, pxa, pua, pxb, pub, pxc, puc, pta, ptb, ptc,
    sx, su, xr, ur, f1, f2, hid, dg, du, rr, tt, wgrad, crecv, yrecv, zlrecv, own,
    zsend, zrecv, send_sem, recv_sem, load_sem,
):
    tokn, feat = tok.shape
    hsize = wg.shape[1]
    ct = feat // 8
    ht = hsize // 3
    half = feat // 2
    hh = hsize // 2
    ra, rb = up16(cap), up16(2 * cap)
    rows = {"A": ra, "B": rb, "C": ra}
    off = {"A": 0, "B": 4 * ra, "C": 4 * (ra + rb)}
    soff = {"A": 0, "B": 3 * ra, "C": 3 * (ra + rb)}

    dp = lax.axis_index("dp")
    ex = lax.axis_index("expert")
    x, z = ex // NZ, ex % NZ
    core = dp % NC
    y = (dp // NC) % NY
    zl = dp // (NC * NY)

    def at_ex(dx, dz):
        return (dp, ((x + dx) % NX) * NZ + (z + dz) % NZ)

    def at_dp(dzl, dy, dc):
        return ((((zl + dzl) % NZL) * NY + (y + dy) % NY) * NC + (core + dc) % NC, ex)

    zup, zdown = at_ex(0, 1), at_ex(0, 3)
    yup, ydown = at_dp(0, 1, 0), at_dp(0, 3, 0)
    other, lopeer = at_dp(0, 0, 1), at_dp(1, 0, 0)

    loads = [
        pltpu.make_async_copy(wg_any, wg, load_sem.at[0]),
        pltpu.make_async_copy(wu_any, wu, load_sem.at[1]),
        pltpu.make_async_copy(wd_any, wd, load_sem.at[2]),
    ]
    for load in loads:
        load.start()

    peers = [zup, zdown, at_ex(1, 0), at_ex(2, 0), at_ex(3, 0), yup, ydown, other, lopeer]
    barrier = pltpu.get_barrier_semaphore()
    for peer in peers:
        pl.semaphore_signal(barrier, inc=1, device_id=peer, device_id_type=MESH)
    pl.semaphore_wait(barrier, len(peers))

    started = []

    def send(src, dst, target):
        number = len(started)
        copy = pltpu.make_async_remote_copy(
            src_ref=src, dst_ref=dst, send_sem=send_sem.at[number], recv_sem=recv_sem.at[number],
            device_id=target, device_id_type=MESH,
        )
        copy.start()
        started.append(copy)
        return copy

    def rws(start, count):
        return pl.ds(start, count)

    g_down = send(gcode, gz.at[0], zdown)
    g_up = send(gcode, gz.at[1], zup)
    t_down = send(tok, zt.at[rws(0, tokn)], zdown)
    t_up = send(tok, zt.at[rws(tokn, tokn)], zup)
    c_down = send(cot, zc.at[rws(0, tokn)], zdown)
    c_up = send(cot, zc.at[rws(tokn, tokn)], zup)

    earlier = (
        lax.broadcasted_iota(jnp.int32, (tokn, tokn), 0)
        < lax.broadcasted_iota(jnp.int32, (tokn, tokn), 1)
    ).astype(BF16)

    def rank(number, codes):
        hits = (codes > 0).astype(BF16)
        slots[number] = jnp.dot(hits, earlier, preferred_element_type=F32)

    def place(number, codes, count, base, px, pu, columns):
        places = lax.broadcasted_iota(jnp.int32, (count, tokn), 0).astype(F32)
        for k in range(NX):
            e = ((x + k) % NX) * NZ + z
            slot_row = slots[number, pl.ds(e, 1), :] + float(base)
            code_row = codes[pl.ds(e, 1), :]
            here = (places == slot_row) & (code_row > 0)
            px[rws(k * count, count), columns] = jnp.where(here, 1.0, 0.0).astype(BF16)
            pu[rws(k * count, count), columns] = jnp.where(here, code_row * (1.0 / 16.0), 0.0).astype(BF16)

    def select(chunk, placer, source, first, depth, stage, out):
        n = rows[chunk]
        picks = placer[...]

        @pl.loop(0, 8)
        def _(j):
            cols = pl.ds(pl.multiple_of(j * ct, ct), ct)
            got = jnp.dot(picks, source[rws(first, depth), cols], preferred_element_type=F32).astype(BF16)
            out[rws(off[chunk], n), cols] = got[:n]
            stage[rws(soff[chunk], 3 * n), cols] = got[n:]

    def spread(chunk, stage, out):
        n = rows[chunk]
        return [
            send(stage.at[rws(soff[chunk] + (k - 1) * n, n)], out.at[rws(off[chunk] + k * n, n)], at_ex(k, 0))
            for k in (2, 1, 3)
        ]

    def arrive(copies):
        for copy in copies:
            copy.wait_recv()

    def gone(copies):
        for copy in copies:
            copy.wait_send()

    def front_x(chunk):
        n = 4 * rows[chunk]
        at = rws(off[chunk], n)

        @pl.loop(0, 3)
        def _(j):
            cols = pl.ds(pl.multiple_of(j * ht, ht), ht)
            gate = jnp.dot(xr[at, :], wg[:, cols], preferred_element_type=F32)
            upv = jnp.dot(xr[at, :], wu[:, cols], preferred_element_type=F32)
            sig = jax.nn.sigmoid(gate)
            active = gate * sig
            f1[at, cols] = upv * sig * (1.0 + gate * (1.0 - sig))
            f2[at, cols] = active
            hid[at, cols] = (active * upv).astype(BF16)

    def front_u(chunk):
        n = 4 * rows[chunk]
        at = rws(off[chunk], n)

        @pl.loop(0, 3)
        def _(j):
            cols = pl.ds(pl.multiple_of(j * ht, ht), ht)
            dh = lax.dot_general(ur[at, :], wd[cols, :], NT, preferred_element_type=F32)
            dg[at, cols] = (dh * f1[at, cols]).astype(BF16)
            du[at, cols] = (dh * f2[at, cols]).astype(BF16)

    def back_rows(chunk):
        n = rows[chunk]
        at = rws(off[chunk], 4 * n)

        @pl.loop(0, 8)
        def _(j):
            cols = pl.ds(pl.multiple_of(j * ct, ct), ct)
            got = lax.dot_general(dg[at, :], wg[cols, :], NT, preferred_element_type=F32)
            got = got + lax.dot_general(du[at, :], wu[cols, :], NT, preferred_element_type=F32)
            got = got.astype(BF16)
            rr[rws(off[chunk], n), cols] = got[:n]
            sx[rws(soff[chunk], 3 * n), cols] = got[n:]

    def give_back(chunk):
        n = rows[chunk]
        return [
            send(
                sx.at[rws(soff[chunk] + (k - 1) * n, n)], rr.at[rws(off[chunk] + k * n, n)],
                at_ex(NX - k, 0),
            )
            for k in (2, 1, 3)
        ]

    rank(0, gcode[...])
    place(0, gcode, ra, 0, pxa, pua, pl.ds(0, tokn))
    select("A", pxa, tok, 0, tokn, sx, xr)
    x_a = spread("A", sx, xr)
    select("A", pua, cot, 0, tokn, su, ur)
    u_a = spread("A", su, ur)

    arrive([g_down, g_up])
    g_far = send(gz.at[1], gz.at[2], zup)
    rank(1, gz[0])
    rank(2, gz[1])
    place(1, gz.at[0], rb, 0, pxb, pub, pl.ds(0, tokn))
    place(2, gz.at[1], rb, cap, pxb, pub, pl.ds(tokn, tokn))
    pta[...] = pxa[...].astype(F32).T.astype(BF16)
    ptb[...] = pxb[...].astype(F32).T.astype(BF16)
    for load in loads:
        load.wait()
    arrive(x_a)
    front_x("A")

    fh = tokn // 2
    arrive([t_down, t_up])
    tf_up = send(zt.at[rws(tokn, fh)], zt.at[rws(2 * tokn, fh)], zup)
    tf_down = send(zt.at[rws(fh, fh)], zt.at[rws(2 * tokn + fh, fh)], zdown)
    select("B", pxb, zt, 0, 2 * tokn, sx, xr)
    x_b = spread("B", sx, xr)

    arrive([c_down, c_up])
    cf_up = send(zc.at[rws(tokn, fh)], zc.at[rws(2 * tokn, fh)], zup)
    cf_down = send(zc.at[rws(fh, fh)], zc.at[rws(2 * tokn + fh, fh)], zdown)
    select("B", pub, zc, 0, 2 * tokn, su, ur)
    u_b = spread("B", su, ur)

    arrive([g_far])
    rank(3, gz[2])
    place(3, gz.at[2], ra, 0, pxc, puc, pl.ds(0, tokn))
    ptc[...] = pxc[...].astype(F32).T.astype(BF16)
    arrive(u_a)
    front_u("A")
    arrive(x_b)
    front_x("B")

    arrive([tf_up, tf_down])
    select("C", pxc, zt, 2 * tokn, tokn, sx, xr)
    x_c = spread("C", sx, xr)
    arrive(u_b)
    front_u("B")
    gone(x_b)
    back_rows("B")

    arrive([cf_up, cf_down])
    select("C", puc, zc, 2 * tokn, tokn, su, ur)
    u_c = spread("C", su, ur)
    r_b = give_back("B")
    gone(x_a)
    back_rows("A")
    arrive(x_c)
    front_x("C")

    def partial(pt, first, chunk, lo):
        n = 4 * rows[chunk]
        return jnp.dot(
            pt[rws(first, tokn), :], rr[rws(off[chunk], n), lo : lo + half],
            preferred_element_type=F32,
        )

    arrive(u_c)
    front_u("C")
    gone(x_c)
    back_rows("C")
    r_c = give_back("C")
    arrive(r_b)
    zsend[0] = partial(ptb, 0, "B", half).astype(BF16)
    z0 = send(zsend.at[0], zrecv.at[0], zup)
    zsend[1] = partial(ptb, tokn, "B", 0).astype(BF16)
    z1 = send(zsend.at[1], zrecv.at[1], zdown)

    def weight_grad(piece, left, right):
        tt[...] = left[...].T

        @pl.loop(0, 8)
        def _(j):
            cols = pl.ds(pl.multiple_of(j * ct, ct), ct)
            got = jnp.dot(tt[...], right[:, cols], preferred_element_type=F32).astype(BF16)
            for c in range(NC):
                for h in range(2):
                    wgrad[c, piece, j % NY, h, j // NY] = got[
                        h * hh : (h + 1) * hh, c * (ct // 2) : (c + 1) * (ct // 2)
                    ]

        return send(wgrad.at[1 - core, piece], crecv.at[piece], other)

    w_0 = weight_grad(0, hid, ur)
    arrive(r_c)
    zsend[2] = partial(ptc, 0, "C", 0).astype(BF16)
    z2 = send(zsend.at[2], zrecv.at[2], zup)
    zsend[3] = partial(ptc, 0, "C", half).astype(BF16)
    z3 = send(zsend.at[3], zrecv.at[3], zdown)
    r_a = give_back("A")
    w_1 = weight_grad(1, dg, xr)
    w_2 = weight_grad(2, du, xr)

    def summed(piece, yi, h, lo):
        return wgrad[core, piece, yi, h, lo].astype(F32) + crecv[piece, yi, h, lo].astype(F32)

    ring = {}

    def ring_step(step, piece):
        for h in range(2):
            yi = (y + NY - 1 - step) % NY if h == 0 else (y + 1 + step) % NY
            if step > 0:
                ring[step - 1, piece, h].wait_recv()

            for lo in range(NZL):
                total = summed(piece, yi, h, lo)
                if step > 0:
                    total = total + yrecv[step - 1, piece, h, lo].astype(F32)
                wgrad[core, piece, yi, h, lo] = total.astype(BF16)
            ring[step, piece, h] = send(
                wgrad.at[core, piece, yi, h], yrecv.at[step, piece, h], yup if h == 0 else ydown
            )

    last = {}

    def lo_step(piece):
        for h in range(2):
            ring[NY - 2, piece, h].wait_recv()
            away = summed(piece, y, h, 1 - zl) + yrecv[NY - 2, piece, h, 1 - zl].astype(F32)
            wgrad[core, piece, y, h, 1 - zl] = away.astype(BF16)
            last[piece, h] = send(wgrad.at[core, piece, y, h, 1 - zl], zlrecv.at[piece, h], lopeer)
            own[piece, h] = summed(piece, y, h, zl) + yrecv[NY - 2, piece, h, zl].astype(F32)

    def finish(piece):
        for h in range(2):
            last[piece, h].wait_recv()
            total = own[piece, h] + zlrecv[piece, h].astype(F32)
            if piece == 0:
                gd_out[pl.ds(h * hh, hh), :] = total
            else:
                out = gg_out if piece == 1 else gu_out
                out[:, h * hh : (h + 1) * hh] = total.T

    arrive([w_0])
    ring_step(0, 0)
    arrive([w_1])
    ring_step(0, 1)
    arrive([w_2])
    ring_step(0, 2)
    arrive([z2])
    zsend[4] = (partial(ptb, 0, "B", 0) + zrecv[2].astype(F32)).astype(BF16)
    z4 = send(zsend.at[4], zrecv.at[4], zup)
    arrive([z3])
    zsend[5] = (partial(ptb, tokn, "B", half) + zrecv[3].astype(F32)).astype(BF16)
    z5 = send(zsend.at[5], zrecv.at[5], zdown)
    for piece in range(3):
        ring_step(1, piece)
    for piece in range(3):
        ring_step(2, piece)
    arrive(r_a)
    arrive([z0, z1, z4, z5])
    gt_out[:, :half] = (
        partial(pta, 0, "A", 0) + zrecv[1].astype(F32) + zrecv[4].astype(F32)
    ).astype(BF16)
    gt_out[:, half:] = (
        partial(pta, 0, "A", half) + zrecv[0].astype(F32) + zrecv[5].astype(F32)
    ).astype(BF16)
    for piece in range(3):
        lo_step(piece)
    for piece in range(3):
        finish(piece)

    already = [*x_a, *x_b, *x_c]
    for copy in started:
        if not any(copy is one for one in already):
            copy.wait_send()


def on_device(tokens, cotangent, expert_ids, gate_codes, gate_weight, up_weight, down_weight):
    experts = NX * NZ
    tokn, feat = tokens.shape
    hsize = gate_weight.shape[2]
    cap = tokn * TOP * 17 // (experts * 16)
    ra, rb = up16(cap), up16(2 * cap)
    nrows = 8 * ra + 4 * rb
    nsend = 6 * ra + 3 * rb
    hh, ds = hsize // 2, feat // 16
    same = expert_ids.T[None, :, :] == jnp.arange(experts, dtype=jnp.int32)[:, None, None]
    codes = jnp.sum(jnp.where(same, gate_codes.T[None, :, :].astype(F32), 0.0), axis=1)
    vmem = pl.BlockSpec(memory_space=pltpu.VMEM)
    anyw = pl.BlockSpec(memory_space=pl.ANY)
    v = pltpu.VMEM
    copies = 71
    outs = pl.pallas_call(
        functools.partial(kernel, cap),
        out_shape=[
            jax.ShapeDtypeStruct((tokn, feat), BF16),
            jax.ShapeDtypeStruct((ds, hsize), F32),
            jax.ShapeDtypeStruct((ds, hsize), F32),
            jax.ShapeDtypeStruct((hsize, ds), F32),
        ],
        in_specs=[vmem] * 3 + [anyw] * 3,
        out_specs=[vmem] * 4,
        scratch_shapes=[
            v((feat, hsize), BF16), v((feat, hsize), BF16), v((hsize, feat), BF16),
            v((3, experts, tokn), F32), v((3 * tokn, feat), BF16), v((3 * tokn, feat), BF16),
            v((4, experts, tokn), F32),
            v((4 * ra, tokn), BF16), v((4 * ra, tokn), BF16),
            v((4 * rb, 2 * tokn), BF16), v((4 * rb, 2 * tokn), BF16),
            v((4 * ra, tokn), BF16), v((4 * ra, tokn), BF16),
            v((tokn, 4 * ra), BF16), v((2 * tokn, 4 * rb), BF16), v((tokn, 4 * ra), BF16),
            v((nsend, feat), BF16), v((nsend, feat), BF16),
            v((nrows, feat), BF16), v((nrows, feat), BF16),
            v((nrows, hsize), F32), v((nrows, hsize), F32),
            v((nrows, hsize), BF16), v((nrows, hsize), BF16), v((nrows, hsize), BF16),
            v((nrows, feat), BF16),
            v((hsize, nrows), BF16),
            v((NC, 3, NY, 2, NZL, hh, ds), BF16),
            v((3, NY, 2, NZL, hh, ds), BF16),
            v((NY - 1, 3, 2, NZL, hh, ds), BF16),
            v((3, 2, hh, ds), BF16),
            v((3, 2, hh, ds), F32),
            v((6, tokn, feat // 2), BF16), v((6, tokn, feat // 2), BF16),
            pltpu.SemaphoreType.DMA((copies,)),
            pltpu.SemaphoreType.DMA((copies,)),
            pltpu.SemaphoreType.DMA((3,)),
        ],
        compiler_params=pltpu.CompilerParams(
            collective_id=0, has_side_effects=True, vmem_limit_bytes=65_000_000
        ),
    )(tokens, cotangent, codes, gate_weight[0], up_weight[0], down_weight[0])
    grad_tokens, grad_gate, grad_up, grad_down = outs
    return (grad_tokens, grad_gate[None], grad_up[None], grad_down[None])


def solution(mesh):
    in_specs = (
        P(("dp", "expert"), None),
        P(("dp", "expert"), None),
        P(("dp", "expert"), None),
        P(("dp", "expert"), None),
        P("expert", None, None),
        P("expert", None, None),
        P("expert", None, None),
    )
    out_specs = (
        P(("dp", "expert"), None),
        P("expert", "dp", None),
        P("expert", "dp", None),
        P("expert", None, "dp"),
    )
    return jax.shard_map(
        on_device, mesh=mesh, in_specs=in_specs, out_specs=out_specs, check_vma=False
    )
```

time: 365 us -> 189 us (0.52)
  Pallas kernels: 0 us -> 178 us
  waiting for transfers between devices: 157 us -> 0 us
  blocking collectives: 93.2 us -> 0 us
  matrix products: 46.2 us -> 0 us
  starting transfers between devices: 21.1 us -> 0 us
  between operations: 14.2 us -> 0.64 us
  local copies, waits for them, and re-layouts: 19.1 us -> 7.18 us
  other arithmetic: 9.91 us -> 1.97 us
    pallas_call x0 -> x1, Pallas kernels: none -> 178 us  [on_device(): pl.pallas_call(functools.partial(kernel, cap), out_shape=[jax.ShapeDtypeS...]
    all_to_all x1 -> x0, blocking collectives: 93.2 us -> none  [on_device(): lax.all_to_all(row_grads, 'expert', split_axis=0, concat_axis=0, tiled=True)]
    all_to_all x2 -> x0, waiting for transfers between devices: 88.3 us -> none  [the longest x1 49.9 us: on_device(): lax.all_to_all(send_tokens, 'expert', split_axis=0, concat_axis=0, tiled=...]
    reduce_scatter x1 -> x0, waiting for transfers between devices: 69.1 us -> none  [on_device(): lax.psum_scatter(jnp.concatenate([jnp.concatenate([gate_part, up_part], a...]
    dot_general x11 -> x0, matrix products: 46.2 us -> none  [the longest x1 5.8 us: down_terms(): jnp.einsum('slcd,slch->dlh', u_rows, hidden, preferred_element_type=jnp.f...]
    all_to_all x2 -> x0, starting transfers between devices: 20.9 us -> none  [the longest x1 11.6 us: on_device(): lax.all_to_all(send_tokens, 'expert', split_axis=0, concat_axis=0, tiled=...]
    reshape x3 -> x0, local copies, waits for them, and re-layouts: 12.5 us -> none  [the longest x1 4.21 us: on_device(): returned_flat = returned.reshape(experts * capacity, features)]
    concatenate x1 -> x0, other arithmetic: 7 us -> none  [on_device(): jnp.concatenate([jnp.concatenate([gate_part, up_part], axis=2), down_term...]
  transfers between devices with their start and end apart: 3 -> 0, of which waited for: 3 -> 0; matrix products, arithmetic and copies ran while one was open for 9% -> 0% of each run, Pallas kernels for 0% -> 0%
where the time goes in v1:
time: 189 us; the launch traced here: 187 us
  Pallas kernels  178 us (94%)
  local copies, waits for them, and re-layouts  7.18 us (4%)
  other arithmetic  1.97 us (1%)
    pallas_call x1, Pallas kernels, on_device(): pl.pallas_call(functools.partial(kernel, cap), out_shape=[jax.ShapeDtypeS...  178 us
    unnamed x4, local copies, waits for them, and re-layouts  7.18 us

profile of v1, /device:TPU:1, one launch (start us, length us, event | category | flops | bytes accessed | tf_op | source)
XLA Modules:
  0.0 187.4 jit_solution(14282281326920777765)
XLA Ops:
  0.6 0.7 convert_bitcast_fusion
  1.3 1.3 select_reduce_fusion.gcode
  2.6 177.6 %shard_map.102 = (bf16[128,2048]{1,0:T(8,128)(2,1)}, f32[128,768]{1,0:T(8,128)}, f32[128,768]{1,0:T(8,128)}, f32[768,128]{1,0:T(8,128)}) custom-call(bf16[128,2048]{1,0:T(8,128)(2,1)} %tok.1, bf16[128,2048]{1,0:T(8,128)(2,1)} %cot.1, f32[16,128]{1,0:T(8,128)} %select_reduce_fusion.gcode, bf16[2048,768]{1,0:T(8,128)(2,1)} %bitcast.9, ...), custom_call_target="tpu_custom_call" | custom-call | tf_op jit(solution)/shard_map/pallas_call | solution.py:379
  180.2 1.9 %copy.15 = bf16[128,2048]{1,0:T(8,128)(2,1)} copy(bf16[128,2048]{1,0:T(8,128)(2,1)} %get-tuple-element.16) | data formatting | bytes 1048576
  182.1 1.8 copy.16
  183.9 1.8 copy.17
  185.6 1.8 copy.18

commit v2 on v1

--- a/solution.py
+++ b/solution.py
@@ -20,9 +20,9 @@
 
 
 def kernel(
-    cap, tok, cot, gcode, wg_any, wu_any, wd_any,
+    cap, tok, cot, ids, wts, wg_any, wu_any, wd_any,
     gt_out, gg_out, gu_out, gd_out,
-    wg, wu, wd, gz, zt, zc, slots, pxa, pua, pxb, pub, pxc, puc, pta, ptb, ptc,
+    gcode, wg, wu, wd, gz, zt, zc, slots, pxa, pua, pxb, pub, pxc, puc, pta, ptb, ptc,
     sx, su, xr, ur, f1, f2, hid, dg, du, rr, tt, wgrad, crecv, yrecv, zlrecv, own,
     zsend, zrecv, send_sem, recv_sem, load_sem,
 ):
@@ -32,6 +32,7 @@
     ht = hsize // 3
     half = feat // 2
     hh = hsize // 2
+    fh = tokn // 2
     ra, rb = up16(cap), up16(2 * cap)
     rows = {"A": ra, "B": rb, "C": ra}
     off = {"A": 0, "B": 4 * ra, "C": 4 * (ra + rb)}
@@ -83,12 +84,29 @@
     def rws(start, count):
         return pl.ds(start, count)
 
+    number = lax.broadcasted_iota(jnp.int32, (NX * NZ, tokn), 0)
+    codes = jnp.zeros((NX * NZ, tokn), F32)
+    for k in range(TOP):
+        codes = codes + jnp.where(number == ids[k : k + 1, :], wts[k : k + 1, :].astype(F32), 0.0)
+    gcode[...] = codes
+
     g_down = send(gcode, gz.at[0], zdown)
     g_up = send(gcode, gz.at[1], zup)
     t_down = send(tok, zt.at[rws(0, tokn)], zdown)
     t_up = send(tok, zt.at[rws(tokn, tokn)], zup)
-    c_down = send(cot, zc.at[rws(0, tokn)], zdown)
-    c_up = send(cot, zc.at[rws(tokn, tokn)], zup)
+
+    def cot_near(side):
+        cols = pl.ds(side * half, half)
+        return [
+            send(cot.at[:, cols], zc.at[rws(0, tokn), cols], zdown),
+            send(cot.at[:, cols], zc.at[rws(tokn, tokn), cols], zup),
+        ]
+
+    def far(buf, cols):
+        return [
+            send(buf.at[rws(tokn, fh), cols], buf.at[rws(2 * tokn, fh), cols], zup),
+            send(buf.at[rws(fh, fh), cols], buf.at[rws(2 * tokn + fh, fh), cols], zdown),
+        ]
 
     earlier = (
         lax.broadcasted_iota(jnp.int32, (tokn, tokn), 0)
@@ -109,23 +127,33 @@
             px[rws(k * count, count), columns] = jnp.where(here, 1.0, 0.0).astype(BF16)
             pu[rws(k * count, count), columns] = jnp.where(here, code_row * (1.0 / 16.0), 0.0).astype(BF16)
 
-    def select(chunk, placer, source, first, depth, stage, out):
+    def select(chunk, placer, source, first, depth, stage, out, tiles=(0, 8)):
         n = rows[chunk]
         picks = placer[...]
 
-        @pl.loop(0, 8)
+        @pl.loop(*tiles)
         def _(j):
             cols = pl.ds(pl.multiple_of(j * ct, ct), ct)
             got = jnp.dot(picks, source[rws(first, depth), cols], preferred_element_type=F32).astype(BF16)
             out[rws(off[chunk], n), cols] = got[:n]
             stage[rws(soff[chunk], 3 * n), cols] = got[n:]
 
-    def spread(chunk, stage, out):
+    whole = pl.ds(0, feat)
+    sides = (pl.ds(0, half), pl.ds(half, half))
+
+    def spread(chunk, stage, out, cols=whole):
         n = rows[chunk]
         return [
-            send(stage.at[rws(soff[chunk] + (k - 1) * n, n)], out.at[rws(off[chunk] + k * n, n)], at_ex(k, 0))
+            send(
+                stage.at[rws(soff[chunk] + (k - 1) * n, n), cols],
+                out.at[rws(off[chunk] + k * n, n), cols], at_ex(k, 0),
+            )
             for k in (2, 1, 3)
         ]
+
+    def spread_cot(chunk, placer, first, depth, side):
+        select(chunk, placer, zc, first, depth, su, ur, (4 * side, 4 * side + 4))
+        return spread(chunk, su, ur, sides[side])
 
     def arrive(copies):
         for copy in copies:
@@ -199,49 +227,49 @@
     place(2, gz.at[1], rb, cap, pxb, pub, pl.ds(tokn, tokn))
     pta[...] = pxa[...].astype(F32).T.astype(BF16)
     ptb[...] = pxb[...].astype(F32).T.astype(BF16)
+    arrive([g_far])
+    rank(3, gz[2])
+    place(3, gz.at[2], ra, 0, pxc, puc, pl.ds(0, tokn))
+    ptc[...] = pxc[...].astype(F32).T.astype(BF16)
     for load in loads:
         load.wait()
     arrive(x_a)
     front_x("A")
 
-    fh = tokn // 2
     arrive([t_down, t_up])
-    tf_up = send(zt.at[rws(tokn, fh)], zt.at[rws(2 * tokn, fh)], zup)
-    tf_down = send(zt.at[rws(fh, fh)], zt.at[rws(2 * tokn + fh, fh)], zdown)
+    t_far = far(zt, whole)
+    c_0 = cot_near(0)
     select("B", pxb, zt, 0, 2 * tokn, sx, xr)
     x_b = spread("B", sx, xr)
-
-    arrive([c_down, c_up])
-    cf_up = send(zc.at[rws(tokn, fh)], zc.at[rws(2 * tokn, fh)], zup)
-    cf_down = send(zc.at[rws(fh, fh)], zc.at[rws(2 * tokn + fh, fh)], zdown)
-    select("B", pub, zc, 0, 2 * tokn, su, ur)
-    u_b = spread("B", su, ur)
-
-    arrive([g_far])
-    rank(3, gz[2])
-    place(3, gz.at[2], ra, 0, pxc, puc, pl.ds(0, tokn))
-    ptc[...] = pxc[...].astype(F32).T.astype(BF16)
     arrive(u_a)
     front_u("A")
+    gone(x_a)
+    back_rows("A")
     arrive(x_b)
     front_x("B")
 
-    arrive([tf_up, tf_down])
+    arrive(t_far)
     select("C", pxc, zt, 2 * tokn, tokn, sx, xr)
     x_c = spread("C", sx, xr)
+    gone(c_0)
+    c_1 = cot_near(1)
+    arrive(c_0)
+    u_b = spread_cot("B", pub, 0, 2 * tokn, 0)
+    arrive(x_c)
+    front_x("C")
+    gone(c_1)
+    c_far0 = far(zc, sides[0])
+    arrive(c_1)
+    c_far1 = far(zc, sides[1])
+    u_b += spread_cot("B", pub, 0, 2 * tokn, 1)
+    arrive(c_far0)
+    u_c = spread_cot("C", puc, 2 * tokn, tokn, 0)
     arrive(u_b)
     front_u("B")
+    arrive(c_far1)
+    u_c += spread_cot("C", puc, 2 * tokn, tokn, 1)
     gone(x_b)
     back_rows("B")
-
-    arrive([cf_up, cf_down])
-    select("C", puc, zc, 2 * tokn, tokn, su, ur)
-    u_c = spread("C", su, ur)
-    r_b = give_back("B")
-    gone(x_a)
-    back_rows("A")
-    arrive(x_c)
-    front_x("C")
 
     def partial(pt, first, chunk, lo):
         n = 4 * rows[chunk]
@@ -249,17 +277,6 @@
             pt[rws(first, tokn), :], rr[rws(off[chunk], n), lo : lo + half],
             preferred_element_type=F32,
         )
-
-    arrive(u_c)
-    front_u("C")
-    gone(x_c)
-    back_rows("C")
-    r_c = give_back("C")
-    arrive(r_b)
-    zsend[0] = partial(ptb, 0, "B", half).astype(BF16)
-    z0 = send(zsend.at[0], zrecv.at[0], zup)
-    zsend[1] = partial(ptb, tokn, "B", 0).astype(BF16)
-    z1 = send(zsend.at[1], zrecv.at[1], zdown)
 
     def weight_grad(piece, left, right):
         tt[...] = left[...].T
@@ -276,16 +293,6 @@
 
         return send(wgrad.at[1 - core, piece], crecv.at[piece], other)
 
-    w_0 = weight_grad(0, hid, ur)
-    arrive(r_c)
-    zsend[2] = partial(ptc, 0, "C", 0).astype(BF16)
-    z2 = send(zsend.at[2], zrecv.at[2], zup)
-    zsend[3] = partial(ptc, 0, "C", half).astype(BF16)
-    z3 = send(zsend.at[3], zrecv.at[3], zdown)
-    r_a = give_back("A")
-    w_1 = weight_grad(1, dg, xr)
-    w_2 = weight_grad(2, du, xr)
-
     def summed(piece, yi, h, lo):
         return wgrad[core, piece, yi, h, lo].astype(F32) + crecv[piece, yi, h, lo].astype(F32)
 
@@ -326,22 +333,45 @@
                 out = gg_out if piece == 1 else gu_out
                 out[:, h * hh : (h + 1) * hh] = total.T
 
+    arrive(u_c)
+    r_b = give_back("B")
+    front_u("C")
+    w_0 = weight_grad(0, hid, ur)
+    gone(x_c)
+    back_rows("C")
+    r_c = give_back("C")
+    r_a = give_back("A")
+    w_1 = weight_grad(1, dg, xr)
     arrive([w_0])
     ring_step(0, 0)
+    w_2 = weight_grad(2, du, xr)
     arrive([w_1])
     ring_step(0, 1)
+    arrive(r_b)
+    zsend[0] = partial(ptb, 0, "B", half).astype(BF16)
+    z0 = send(zsend.at[0], zrecv.at[0], zup)
+    zsend[1] = partial(ptb, tokn, "B", 0).astype(BF16)
+    z1 = send(zsend.at[1], zrecv.at[1], zdown)
     arrive([w_2])
     ring_step(0, 2)
-    arrive([z2])
+    ring_step(1, 0)
+    ring_step(1, 1)
+    arrive(r_c)
+    zsend[2] = partial(ptc, 0, "C", 0).astype(BF16)
+    z2 = send(zsend.at[2], zrecv.at[2], zup)
+    zsend[3] = partial(ptc, 0, "C", half).astype(BF16)
+    z3 = send(zsend.at[3], zrecv.at[3], zdown)
+    ring_step(1, 2)
+    ring_step(2, 0)
+    arrive([z2, z3])
     zsend[4] = (partial(ptb, 0, "B", 0) + zrecv[2].astype(F32)).astype(BF16)
     z4 = send(zsend.at[4], zrecv.at[4], zup)
-    arrive([z3])
     zsend[5] = (partial(ptb, tokn, "B", half) + zrecv[3].astype(F32)).astype(BF16)
     z5 = send(zsend.at[5], zrecv.at[5], zdown)
+    ring_step(2, 1)
+    ring_step(2, 2)
     for piece in range(3):
-        ring_step(1, piece)
-    for piece in range(3):
-        ring_step(2, piece)
+        lo_step(piece)
     arrive(r_a)
     arrive([z0, z1, z4, z5])
     gt_out[:, :half] = (
@@ -351,14 +381,32 @@
         partial(pta, 0, "A", half) + zrecv[0].astype(F32) + zrecv[5].astype(F32)
     ).astype(BF16)
     for piece in range(3):
-        lo_step(piece)
-    for piece in range(3):
         finish(piece)
 
-    already = [*x_a, *x_b, *x_c]
+    already = [*x_a, *x_b, *x_c, *c_0, *c_1]
     for copy in started:
         if not any(copy is one for one in already):
             copy.wait_send()
+
+
+def hand_on_kernel(*refs):
+    sem = refs[-1]
+    moves = [pltpu.make_async_copy(refs[i], refs[4 + i], sem.at[i]) for i in range(4)]
+    for move in moves:
+        move.start()
+    for move in moves:
+        move.wait()
+
+
+def hand_on(arrays):
+    return pl.pallas_call(
+        hand_on_kernel,
+        out_shape=[jax.ShapeDtypeStruct(a.shape, a.dtype) for a in arrays],
+        in_specs=[pl.BlockSpec(memory_space=pl.ANY)] * 4,
+        out_specs=[pl.BlockSpec(memory_space=pl.ANY)] * 4,
+        scratch_shapes=[pltpu.SemaphoreType.DMA((4,))],
+        compiler_params=pltpu.CompilerParams(vmem_limit_bytes=65_000_000),
+    )(*arrays)
 
 
 def on_device(tokens, cotangent, expert_ids, gate_codes, gate_weight, up_weight, down_weight):
@@ -370,12 +418,10 @@
     nrows = 8 * ra + 4 * rb
     nsend = 6 * ra + 3 * rb
     hh, ds = hsize // 2, feat // 16
-    same = expert_ids.T[None, :, :] == jnp.arange(experts, dtype=jnp.int32)[:, None, None]
-    codes = jnp.sum(jnp.where(same, gate_codes.T[None, :, :].astype(F32), 0.0), axis=1)
     vmem = pl.BlockSpec(memory_space=pltpu.VMEM)
     anyw = pl.BlockSpec(memory_space=pl.ANY)
     v = pltpu.VMEM
-    copies = 71
+    copies = 81
     outs = pl.pallas_call(
         functools.partial(kernel, cap),
         out_shape=[
@@ -384,9 +430,10 @@
             jax.ShapeDtypeStruct((ds, hsize), F32),
             jax.ShapeDtypeStruct((hsize, ds), F32),
         ],
-        in_specs=[vmem] * 3 + [anyw] * 3,
+        in_specs=[vmem] * 4 + [anyw] * 3,
         out_specs=[vmem] * 4,
         scratch_shapes=[
+            v((experts, tokn), F32),
             v((feat, hsize), BF16), v((feat, hsize), BF16), v((hsize, feat), BF16),
             v((3, experts, tokn), F32), v((3 * tokn, feat), BF16), v((3 * tokn, feat), BF16),
             v((4, experts, tokn), F32),
@@ -413,7 +460,8 @@
         compiler_params=pltpu.CompilerParams(
             collective_id=0, has_side_effects=True, vmem_limit_bytes=65_000_000
         ),
-    )(tokens, cotangent, codes, gate_weight[0], up_weight[0], down_weight[0])
+    )(tokens, cotangent, expert_ids.T, gate_codes.T, gate_weight[0], up_weight[0], down_weight[0])
+    outs = hand_on(outs)
     grad_tokens, grad_gate, grad_up, grad_down = outs
     return (grad_tokens, grad_gate[None], grad_up[None], grad_down[None])
 

time: 189 us -> 216 us (1.14)
  Pallas kernels: 178 us -> 213 us
  local copies, waits for them, and re-layouts: 7.18 us -> 0 us
    pallas_call x0 -> x1, Pallas kernels: none -> 52.8 us  [hand_on(): pl.pallas_call(hand_on_kernel, out_shape=[jax.ShapeDtypeStruct(a.shape, a...]
    pallas_call x1, Pallas kernels: 178 us -> 160 us  [on_device(): pl.pallas_call(functools.partial(kernel, cap), out_shape=[jax.ShapeDtypeS...]
    unnamed x4 -> x0, local copies, waits for them, and re-layouts: 7.18 us -> none
where the time goes in v2:
time: 216 us; the launch traced here: 214 us
  Pallas kernels  213 us (99%)
    pallas_call x1, Pallas kernels, on_device(): pl.pallas_call(functools.partial(kernel, cap), out_shape=[jax.ShapeDtypeS...  160 us
    pallas_call x1, Pallas kernels, hand_on(): pl.pallas_call(hand_on_kernel, out_shape=[jax.ShapeDtypeStruct(a.shape, a...  52.8 us

profile of v2, /device:TPU:1, one launch (start us, length us, event | category | flops | bytes accessed | tf_op | source)
XLA Modules:
  0.0 213.7 jit_solution(10944663446238987066)
XLA Ops:
  0.6 160.3 %shard_map.102 = (bf16[128,2048]{1,0:T(8,128)(2,1)}, f32[128,768]{1,0:T(8,128)}, f32[128,768]{1,0:T(8,128)}, f32[768,128]{1,0:T(8,128)}) custom-call(bf16[128,2048]{1,0:T(8,128)(2,1)} %tok.1, bf16[128,2048]{1,0:T(8,128)(2,1)} %cot.1, s32[4,128]{1,0:T(4,128)} %bitcast.11, s32[4,128]{1,0:T(4,128)} %bitcast.12, bf16[2048,768]{1,0:T(8,128)(2,1)} %bitcast.8, ...), custom_call_target="tpu_custom_call" | custom-call | tf_op jit(solution)/shard_map/pallas_call | solution.py:425
  160.9 52.8 %shard_map.103 = (bf16[128,2048]{1,0:T(8,128)(2,1)}, f32[128,768]{1,0:T(8,128)}, f32[128,768]{1,0:T(8,128)}, f32[768,128]{1,0:T(8,128)}) custom-call(bf16[128,2048]{1,0:T(8,128)(2,1)} %get-tuple-element.12.refs_0_, f32[128,768]{1,0:T(8,128)} %get-tuple-element.13.refs_1_, f32[128,768]{1,0:T(8,128)} %get-tuple-element.14.refs_2_, ...), custom_call_target="tpu_custom_call" | custom-call | tf_op jit(solution)/shard_map/pallas_call | solution.py:402

commit v3 on v2

--- a/solution.py
+++ b/solution.py
@@ -390,11 +390,15 @@
 
 
 def hand_on_kernel(*refs):
-    sem = refs[-1]
-    moves = [pltpu.make_async_copy(refs[i], refs[4 + i], sem.at[i]) for i in range(4)]
-    for move in moves:
+    given, out, held, sem = refs[:4], refs[4:8], refs[8:12], refs[12]
+    ins = [pltpu.make_async_copy(given[i], held[i], sem.at[i]) for i in range(4)]
+    outs = [pltpu.make_async_copy(held[i], out[i], sem.at[4 + i]) for i in range(4)]
+    for move in ins:
         move.start()
-    for move in moves:
+    for i in range(4):
+        ins[i].wait()
+        outs[i].start()
+    for move in outs:
         move.wait()
 
 
@@ -404,8 +408,8 @@
         out_shape=[jax.ShapeDtypeStruct(a.shape, a.dtype) for a in arrays],
         in_specs=[pl.BlockSpec(memory_space=pl.ANY)] * 4,
         out_specs=[pl.BlockSpec(memory_space=pl.ANY)] * 4,
-        scratch_shapes=[pltpu.SemaphoreType.DMA((4,))],
-        compiler_params=pltpu.CompilerParams(vmem_limit_bytes=65_000_000),
+        scratch_shapes=[pltpu.VMEM(a.shape, a.dtype) for a in arrays] + [pltpu.SemaphoreType.DMA((8,))],
+        compiler_params=pltpu.CompilerParams(vmem_limit_bytes=60_000_000),
     )(*arrays)
 
 

time: 216 us -> 165 us (0.76)
  Pallas kernels: 213 us -> 163 us
    pallas_call x1, Pallas kernels: 52.8 us -> 2.29 us  [hand_on(): pl.pallas_call(hand_on_kernel, out_shape=[jax.ShapeDtypeStruct(a.shape, a...]
where the time goes in v3:
time: 165 us; the launch traced here: 163 us
  Pallas kernels  163 us (99%)
    pallas_call x1, Pallas kernels, on_device(): pl.pallas_call(functools.partial(kernel, cap), out_shape=[jax.ShapeDtypeS...  160 us

profile of v3, /device:TPU:1, one launch (start us, length us, event | category | flops | bytes accessed | tf_op | source)
XLA Modules:
  0.0 163.2 jit_solution(18137642733691256396)
XLA Ops:
  0.6 160.3 %shard_map.102 = (bf16[128,2048]{1,0:T(8,128)(2,1)}, f32[128,768]{1,0:T(8,128)}, f32[128,768]{1,0:T(8,128)}, f32[768,128]{1,0:T(8,128)}) custom-call(bf16[128,2048]{1,0:T(8,128)(2,1)} %tok.1, bf16[128,2048]{1,0:T(8,128)(2,1)} %cot.1, s32[4,128]{1,0:T(4,128)} %bitcast.11, s32[4,128]{1,0:T(4,128)} %bitcast.12, bf16[2048,768]{1,0:T(8,128)(2,1)} %bitcast.8, ...), custom_call_target="tpu_custom_call" | custom-call | tf_op jit(solution)/shard_map/pallas_call | solution.py:429
  160.9 2.3 %shard_map.103 = (bf16[128,2048]{1,0:T(8,128)(2,1)}, f32[128,768]{1,0:T(8,128)}, f32[128,768]{1,0:T(8,128)}, f32[768,128]{1,0:T(8,128)}) custom-call(bf16[128,2048]{1,0:T(8,128)(2,1)} %get-tuple-element.12.refs_0_, f32[128,768]{1,0:T(8,128)} %get-tuple-element.13.refs_1_, f32[128,768]{1,0:T(8,128)} %get-tuple-element.14.refs_2_, ...), custom_call_target="tpu_custom_call" | custom-call | tf_op jit(solution)/shard_map/pallas_call | solution.py:406

commit v4 on v3

--- a/solution.py
+++ b/solution.py
@@ -17,6 +17,11 @@
 
 def up16(n):
     return -(-n // 16) * 16
+
+
+def split_rows(cap):
+    main = cap // 16 * 16
+    return main, up16(cap + 3 * (cap - main))
 
 
 def kernel(
@@ -33,10 +38,11 @@
     half = feat // 2
     hh = hsize // 2
     fh = tokn // 2
-    ra, rb = up16(cap), up16(2 * cap)
-    rows = {"A": ra, "B": rb, "C": ra}
-    off = {"A": 0, "B": 4 * ra, "C": 4 * (ra + rb)}
-    soff = {"A": 0, "B": 3 * ra, "C": 3 * (ra + rb)}
+    main, rc = split_rows(cap)
+    extra = cap - main
+    rows = {"A": main, "B": 2 * main, "C": rc}
+    off = {"A": 0, "B": 4 * main, "C": 12 * main}
+    soff = {"A": 0, "B": 3 * main, "C": 9 * main}
 
     dp = lax.axis_index("dp")
     ex = lax.axis_index("expert")
@@ -117,15 +123,20 @@
         hits = (codes > 0).astype(BF16)
         slots[number] = jnp.dot(hits, earlier, preferred_element_type=F32)
 
-    def place(number, codes, count, base, px, pu, columns):
+    def place(number, codes, count, base, px, pu, columns, least=0, most=cap):
         places = lax.broadcasted_iota(jnp.int32, (count, tokn), 0).astype(F32)
         for k in range(NX):
             e = ((x + k) % NX) * NZ + z
-            slot_row = slots[number, pl.ds(e, 1), :] + float(base)
+            slot_row = slots[number, pl.ds(e, 1), :]
             code_row = codes[pl.ds(e, 1), :]
-            here = (places == slot_row) & (code_row > 0)
+            here = (places == slot_row + float(base)) & (code_row > 0)
+            here = here & (slot_row >= float(least)) & (slot_row < float(most))
             px[rws(k * count, count), columns] = jnp.where(here, 1.0, 0.0).astype(BF16)
             pu[rws(k * count, count), columns] = jnp.where(here, code_row * (1.0 / 16.0), 0.0).astype(BF16)
+
+    def place_extra(number, codes, order, column):
+        base = cap + order * extra - main
+        place(number, codes, rc, base, pxc, puc, pl.ds(column * tokn, tokn), main)
 
     def select(chunk, placer, source, first, depth, stage, out, tiles=(0, 8)):
         n = rows[chunk]
@@ -213,23 +224,28 @@
         ]
 
     rank(0, gcode[...])
-    place(0, gcode, ra, 0, pxa, pua, pl.ds(0, tokn))
+    place(0, gcode, main, 0, pxa, pua, pl.ds(0, tokn), 0, main)
     select("A", pxa, tok, 0, tokn, sx, xr)
     x_a = spread("A", sx, xr)
     select("A", pua, cot, 0, tokn, su, ur)
     u_a = spread("A", su, ur)
+    zt[rws(3 * tokn, tokn), :] = tok[...]
+    zc[rws(3 * tokn, tokn), :] = cot[...]
+    place_extra(0, gcode, 0, 3)
 
     arrive([g_down, g_up])
     g_far = send(gz.at[1], gz.at[2], zup)
     rank(1, gz[0])
     rank(2, gz[1])
-    place(1, gz.at[0], rb, 0, pxb, pub, pl.ds(0, tokn))
-    place(2, gz.at[1], rb, cap, pxb, pub, pl.ds(tokn, tokn))
+    place(1, gz.at[0], 2 * main, 0, pxb, pub, pl.ds(0, tokn), 0, main)
+    place(2, gz.at[1], 2 * main, main, pxb, pub, pl.ds(tokn, tokn), 0, main)
+    place_extra(1, gz.at[0], 1, 0)
+    place_extra(2, gz.at[1], 2, 1)
     pta[...] = pxa[...].astype(F32).T.astype(BF16)
     ptb[...] = pxb[...].astype(F32).T.astype(BF16)
     arrive([g_far])
     rank(3, gz[2])
-    place(3, gz.at[2], ra, 0, pxc, puc, pl.ds(0, tokn))
+    place(3, gz.at[2], rc, 0, pxc, puc, pl.ds(2 * tokn, tokn))
     ptc[...] = pxc[...].astype(F32).T.astype(BF16)
     for load in loads:
         load.wait()
@@ -238,19 +254,19 @@
 
     arrive([t_down, t_up])
     t_far = far(zt, whole)
-    c_0 = cot_near(0)
     select("B", pxb, zt, 0, 2 * tokn, sx, xr)
     x_b = spread("B", sx, xr)
     arrive(u_a)
     front_u("A")
+    gone(t_far)
+    c_0 = cot_near(0)
+    arrive(t_far)
+    select("C", pxc, zt, 0, 4 * tokn, sx, xr)
+    x_c = spread("C", sx, xr)
     gone(x_a)
     back_rows("A")
     arrive(x_b)
     front_x("B")
-
-    arrive(t_far)
-    select("C", pxc, zt, 2 * tokn, tokn, sx, xr)
-    x_c = spread("C", sx, xr)
     gone(c_0)
     c_1 = cot_near(1)
     arrive(c_0)
@@ -260,38 +276,46 @@
     gone(c_1)
     c_far0 = far(zc, sides[0])
     arrive(c_1)
+    u_b += spread_cot("B", pub, 0, 2 * tokn, 1)
+    gone(c_far0)
     c_far1 = far(zc, sides[1])
-    u_b += spread_cot("B", pub, 0, 2 * tokn, 1)
     arrive(c_far0)
-    u_c = spread_cot("C", puc, 2 * tokn, tokn, 0)
+    u_c = spread_cot("C", puc, 0, 4 * tokn, 0)
     arrive(u_b)
     front_u("B")
-    arrive(c_far1)
-    u_c += spread_cot("C", puc, 2 * tokn, tokn, 1)
     gone(x_b)
     back_rows("B")
-
-    def partial(pt, first, chunk, lo):
+    arrive(c_far1)
+    u_c += spread_cot("C", puc, 0, 4 * tokn, 1)
+
+    def product(pt, first, chunk, cols):
         n = 4 * rows[chunk]
         return jnp.dot(
-            pt[rws(first, tokn), :], rr[rws(off[chunk], n), lo : lo + half],
-            preferred_element_type=F32,
+            pt[rws(first, tokn), :], rr[rws(off[chunk], n), cols], preferred_element_type=F32
         )
 
-    def weight_grad(piece, left, right):
-        tt[...] = left[...].T
+    def near_part(order, side):
+        cols = sides[side]
+        return product(ptb, order * tokn, "B", cols) + product(ptc, order * tokn, "C", cols)
+
+    first_rows = 12 * main
+
+    def weight_grad(piece, left, right, late):
+        at = pl.ds(first_rows, 4 * rc) if late else pl.ds(0, first_rows)
+        tt[:, at] = left[at, :].T
 
         @pl.loop(0, 8)
         def _(j):
             cols = pl.ds(pl.multiple_of(j * ct, ct), ct)
-            got = jnp.dot(tt[...], right[:, cols], preferred_element_type=F32).astype(BF16)
+            got = jnp.dot(tt[:, at], right[at, cols], preferred_element_type=F32)
             for c in range(NC):
                 for h in range(2):
-                    wgrad[c, piece, j % NY, h, j // NY] = got[
-                        h * hh : (h + 1) * hh, c * (ct // 2) : (c + 1) * (ct // 2)
-                    ]
-
-        return send(wgrad.at[1 - core, piece], crecv.at[piece], other)
+                    part = got[h * hh : (h + 1) * hh, c * (ct // 2) : (c + 1) * (ct // 2)]
+                    if late:
+                        part = part + wgrad[c, piece, j % NY, h, j // NY].astype(F32)
+                    wgrad[c, piece, j % NY, h, j // NY] = part.astype(BF16)
+
+        return send(wgrad.at[1 - core, piece], crecv.at[piece], other) if late else None
 
     def summed(piece, yi, h, lo):
         return wgrad[core, piece, yi, h, lo].astype(F32) + crecv[piece, yi, h, lo].astype(F32)
@@ -333,57 +357,58 @@
                 out = gg_out if piece == 1 else gu_out
                 out[:, h * hh : (h + 1) * hh] = total.T
 
+    for piece, (left, right) in enumerate(((hid, ur), (dg, xr), (du, xr))):
+        weight_grad(piece, left, right, False)
     arrive(u_c)
-    r_b = give_back("B")
     front_u("C")
-    w_0 = weight_grad(0, hid, ur)
     gone(x_c)
     back_rows("C")
     r_c = give_back("C")
-    r_a = give_back("A")
-    w_1 = weight_grad(1, dg, xr)
+    w_0 = weight_grad(0, hid, ur, True)
+    w_1 = weight_grad(1, dg, xr, True)
+    w_2 = weight_grad(2, du, xr, True)
     arrive([w_0])
     ring_step(0, 0)
-    w_2 = weight_grad(2, du, xr)
     arrive([w_1])
     ring_step(0, 1)
-    arrive(r_b)
-    zsend[0] = partial(ptb, 0, "B", half).astype(BF16)
-    z0 = send(zsend.at[0], zrecv.at[0], zup)
-    zsend[1] = partial(ptb, tokn, "B", 0).astype(BF16)
-    z1 = send(zsend.at[1], zrecv.at[1], zdown)
     arrive([w_2])
     ring_step(0, 2)
+    arrive(r_c)
+    r_b = give_back("B")
+    zsend[2] = product(ptc, 2 * tokn, "C", sides[0]).astype(BF16)
+    z2 = send(zsend.at[2], zrecv.at[2], zup)
+    zsend[3] = product(ptc, 2 * tokn, "C", sides[1]).astype(BF16)
+    z3 = send(zsend.at[3], zrecv.at[3], zdown)
     ring_step(1, 0)
     ring_step(1, 1)
-    arrive(r_c)
-    zsend[2] = partial(ptc, 0, "C", 0).astype(BF16)
-    z2 = send(zsend.at[2], zrecv.at[2], zup)
-    zsend[3] = partial(ptc, 0, "C", half).astype(BF16)
-    z3 = send(zsend.at[3], zrecv.at[3], zdown)
     ring_step(1, 2)
+    arrive(r_b)
+    r_a = give_back("A")
+    zsend[0] = near_part(0, 1).astype(BF16)
+    z0 = send(zsend.at[0], zrecv.at[0], zup)
+    zsend[1] = near_part(1, 0).astype(BF16)
+    z1 = send(zsend.at[1], zrecv.at[1], zdown)
+    arrive([z2, z3])
+    zsend[4] = (near_part(0, 0) + zrecv[2].astype(F32)).astype(BF16)
+    z4 = send(zsend.at[4], zrecv.at[4], zup)
+    zsend[5] = (near_part(1, 1) + zrecv[3].astype(F32)).astype(BF16)
+    z5 = send(zsend.at[5], zrecv.at[5], zdown)
     ring_step(2, 0)
-    arrive([z2, z3])
-    zsend[4] = (partial(ptb, 0, "B", 0) + zrecv[2].astype(F32)).astype(BF16)
-    z4 = send(zsend.at[4], zrecv.at[4], zup)
-    zsend[5] = (partial(ptb, tokn, "B", half) + zrecv[3].astype(F32)).astype(BF16)
-    z5 = send(zsend.at[5], zrecv.at[5], zdown)
     ring_step(2, 1)
     ring_step(2, 2)
     for piece in range(3):
         lo_step(piece)
     arrive(r_a)
     arrive([z0, z1, z4, z5])
-    gt_out[:, :half] = (
-        partial(pta, 0, "A", 0) + zrecv[1].astype(F32) + zrecv[4].astype(F32)
-    ).astype(BF16)
-    gt_out[:, half:] = (
-        partial(pta, 0, "A", half) + zrecv[0].astype(F32) + zrecv[5].astype(F32)
-    ).astype(BF16)
+    for side, parts in ((0, (1, 4)), (1, (0, 5))):
+        total = product(pta, 0, "A", sides[side]) + product(ptc, 3 * tokn, "C", sides[side])
+        for part in parts:
+            total = total + zrecv[part].astype(F32)
+        gt_out[:, sides[side]] = total.astype(BF16)
     for piece in range(3):
         finish(piece)
 
-    already = [*x_a, *x_b, *x_c, *c_0, *c_1]
+    already = [*x_a, *x_b, *x_c, *t_far, *c_0, *c_1, *c_far0]
     for copy in started:
         if not any(copy is one for one in already):
             copy.wait_send()
@@ -418,9 +443,10 @@
     tokn, feat = tokens.shape
     hsize = gate_weight.shape[2]
     cap = tokn * TOP * 17 // (experts * 16)
-    ra, rb = up16(cap), up16(2 * cap)
-    nrows = 8 * ra + 4 * rb
-    nsend = 6 * ra + 3 * rb
+    main, rc = split_rows(cap)
+    ra, rb = main, 2 * main
+    nrows = 12 * main + 4 * rc
+    nsend = 9 * main + 3 * rc
     hh, ds = hsize // 2, feat // 16
     vmem = pl.BlockSpec(memory_space=pltpu.VMEM)
     anyw = pl.BlockSpec(memory_space=pl.ANY)
@@ -439,12 +465,12 @@
         scratch_shapes=[
             v((experts, tokn), F32),
             v((feat, hsize), BF16), v((feat, hsize), BF16), v((hsize, feat), BF16),
-            v((3, experts, tokn), F32), v((3 * tokn, feat), BF16), v((3 * tokn, feat), BF16),
+            v((3, experts, tokn), F32), v((4 * tokn, feat), BF16), v((4 * tokn, feat), BF16),
             v((4, experts, tokn), F32),
             v((4 * ra, tokn), BF16), v((4 * ra, tokn), BF16),
             v((4 * rb, 2 * tokn), BF16), v((4 * rb, 2 * tokn), BF16),
-            v((4 * ra, tokn), BF16), v((4 * ra, tokn), BF16),
-            v((tokn, 4 * ra), BF16), v((2 * tokn, 4 * rb), BF16), v((tokn, 4 * ra), BF16),
+            v((4 * rc, 4 * tokn), BF16), v((4 * rc, 4 * tokn), BF16),
+            v((tokn, 4 * ra), BF16), v((2 * tokn, 4 * rb), BF16), v((4 * tokn, 4 * rc), BF16),
             v((nsend, feat), BF16), v((nsend, feat), BF16),
             v((nrows, feat), BF16), v((nrows, feat), BF16),
             v((nrows, hsize), F32), v((nrows, hsize), F32),

time: 165 us -> 167 us (1.012)
  Pallas kernels: 163 us -> 166 us
    pallas_call x1, Pallas kernels: 160 us -> 163 us  [on_device(): pl.pallas_call(functools.partial(kernel, cap), out_shape=[jax.ShapeDtypeS...]
where the time goes in v4:
time: 167 us; the launch traced here: 166 us
  Pallas kernels  166 us (99%)
    pallas_call x1, Pallas kernels, on_device(): pl.pallas_call(functools.partial(kernel, cap), out_shape=[jax.ShapeDtypeS...  163 us

profile of v4, /device:TPU:1, one launch (start us, length us, event | category | flops | bytes accessed | tf_op | source)
XLA Modules:
  0.0 166.3 jit_solution(14947042238429230995)
XLA Ops:
  0.6 163.4 %shard_map.102 = (bf16[128,2048]{1,0:T(8,128)(2,1)}, f32[128,768]{1,0:T(8,128)}, f32[128,768]{1,0:T(8,128)}, f32[768,128]{1,0:T(8,128)}) custom-call(bf16[128,2048]{1,0:T(8,128)(2,1)} %tok.1, bf16[128,2048]{1,0:T(8,128)(2,1)} %cot.1, s32[4,128]{1,0:T(4,128)} %bitcast.11, s32[4,128]{1,0:T(4,128)} %bitcast.12, bf16[2048,768]{1,0:T(8,128)(2,1)} %bitcast.8, ...), custom_call_target="tpu_custom_call" | custom-call | tf_op jit(solution)/shard_map/pallas_call | solution.py:455
  164.0 2.3 %shard_map.103 = (bf16[128,2048]{1,0:T(8,128)(2,1)}, f32[128,768]{1,0:T(8,128)}, f32[128,768]{1,0:T(8,128)}, f32[768,128]{1,0:T(8,128)}) custom-call(bf16[128,2048]{1,0:T(8,128)(2,1)} %get-tuple-element.12.refs_0_, f32[128,768]{1,0:T(8,128)} %get-tuple-element.13.refs_1_, f32[128,768]{1,0:T(8,128)} %get-tuple-element.14.refs_2_, ...), custom_call_target="tpu_custom_call" | custom-call | tf_op jit(solution)/shard_map/pallas_call | solution.py:431

commit v5 on v4

--- a/solution.py
+++ b/solution.py
@@ -213,14 +213,14 @@
             rr[rws(off[chunk], n), cols] = got[:n]
             sx[rws(soff[chunk], 3 * n), cols] = got[n:]
 
-    def give_back(chunk):
+    def give_back(chunk, ways=(2, 1, 3)):
         n = rows[chunk]
         return [
             send(
                 sx.at[rws(soff[chunk] + (k - 1) * n, n)], rr.at[rws(off[chunk] + k * n, n)],
                 at_ex(NX - k, 0),
             )
-            for k in (2, 1, 3)
+            for k in ways
         ]
 
     rank(0, gcode[...])
@@ -300,113 +300,152 @@
 
     first_rows = 12 * main
 
-    def weight_grad(piece, left, right, late):
-        at = pl.ds(first_rows, 4 * rc) if late else pl.ds(0, first_rows)
+    lows = (1 - zl, zl)
+    early = pl.ds(0, first_rows)
+    late = pl.ds(first_rows, 4 * rc)
+    every = pl.ds(0, first_rows + 4 * rc)
+
+    def turn(left, at):
         tt[:, at] = left[at, :].T
 
-        @pl.loop(0, 8)
+    def weight_grad(piece, right, at, part, add=False):
+        @pl.loop(0, 4)
         def _(j):
-            cols = pl.ds(pl.multiple_of(j * ct, ct), ct)
+            tile = lows[part] * NY + j
+            cols = pl.ds(pl.multiple_of(tile * ct, ct), ct)
             got = jnp.dot(tt[:, at], right[at, cols], preferred_element_type=F32)
             for c in range(NC):
                 for h in range(2):
-                    part = got[h * hh : (h + 1) * hh, c * (ct // 2) : (c + 1) * (ct // 2)]
-                    if late:
-                        part = part + wgrad[c, piece, j % NY, h, j // NY].astype(F32)
-                    wgrad[c, piece, j % NY, h, j // NY] = part.astype(BF16)
-
-        return send(wgrad.at[1 - core, piece], crecv.at[piece], other) if late else None
+                    value = got[h * hh : (h + 1) * hh, c * (ct // 2) : (c + 1) * (ct // 2)]
+                    if add:
+                        value = value + wgrad[c, piece, lows[part], j, h].astype(F32)
+                    wgrad[c, piece, lows[part], j, h] = value.astype(BF16)
+
+    def swap(piece, part):
+        return send(
+            wgrad.at[1 - core, piece, lows[part]], crecv.at[piece, lows[part]], other
+        )
 
     def summed(piece, yi, h, lo):
-        return wgrad[core, piece, yi, h, lo].astype(F32) + crecv[piece, yi, h, lo].astype(F32)
+        return wgrad[core, piece, lo, yi, h].astype(F32) + crecv[piece, lo, yi, h].astype(F32)
 
     ring = {}
 
-    def ring_step(step, piece):
+    def ring_step(step, piece, part):
+        lo = lows[part]
         for h in range(2):
             yi = (y + NY - 1 - step) % NY if h == 0 else (y + 1 + step) % NY
+            total = summed(piece, yi, h, lo)
             if step > 0:
-                ring[step - 1, piece, h].wait_recv()
-
-            for lo in range(NZL):
-                total = summed(piece, yi, h, lo)
-                if step > 0:
-                    total = total + yrecv[step - 1, piece, h, lo].astype(F32)
-                wgrad[core, piece, yi, h, lo] = total.astype(BF16)
-            ring[step, piece, h] = send(
-                wgrad.at[core, piece, yi, h], yrecv.at[step, piece, h], yup if h == 0 else ydown
+                ring[step - 1, piece, part, h].wait_recv()
+                total = total + yrecv[step - 1, piece, lo, h].astype(F32)
+            wgrad[core, piece, lo, yi, h] = total.astype(BF16)
+            ring[step, piece, part, h] = send(
+                wgrad.at[core, piece, lo, yi, h], yrecv.at[step, piece, lo, h],
+                yup if h == 0 else ydown,
             )
 
     last = {}
 
     def lo_step(piece):
         for h in range(2):
-            ring[NY - 2, piece, h].wait_recv()
-            away = summed(piece, y, h, 1 - zl) + yrecv[NY - 2, piece, h, 1 - zl].astype(F32)
-            wgrad[core, piece, y, h, 1 - zl] = away.astype(BF16)
-            last[piece, h] = send(wgrad.at[core, piece, y, h, 1 - zl], zlrecv.at[piece, h], lopeer)
-            own[piece, h] = summed(piece, y, h, zl) + yrecv[NY - 2, piece, h, zl].astype(F32)
+            ring[NY - 2, piece, 0, h].wait_recv()
+            away = summed(piece, y, h, lows[0]) + yrecv[NY - 2, piece, lows[0], h].astype(F32)
+            wgrad[core, piece, lows[0], y, h] = away.astype(BF16)
+            last[piece, h] = send(wgrad.at[core, piece, lows[0], y, h], zlrecv.at[piece, h], lopeer)
 
     def finish(piece):
         for h in range(2):
+            ring[NY - 2, piece, 1, h].wait_recv()
+            total = summed(piece, y, h, lows[1]) + yrecv[NY - 2, piece, lows[1], h].astype(F32)
             last[piece, h].wait_recv()
-            total = own[piece, h] + zlrecv[piece, h].astype(F32)
+            total = total + zlrecv[piece, h].astype(F32)
             if piece == 0:
                 gd_out[pl.ds(h * hh, hh), :] = total
             else:
                 out = gg_out if piece == 1 else gu_out
                 out[:, h * hh : (h + 1) * hh] = total.T
 
-    for piece, (left, right) in enumerate(((hid, ur), (dg, xr), (du, xr))):
-        weight_grad(piece, left, right, False)
+    turn(hid, early)
+    weight_grad(0, ur, early, 0)
+    weight_grad(0, ur, early, 1)
+    turn(hid, late)
     arrive(u_c)
+    r_b = give_back("B", (2,))
     front_u("C")
     gone(x_c)
     back_rows("C")
     r_c = give_back("C")
-    w_0 = weight_grad(0, hid, ur, True)
-    w_1 = weight_grad(1, dg, xr, True)
-    w_2 = weight_grad(2, du, xr, True)
+    weight_grad(0, ur, late, 0, True)
+    w_0 = swap(0, 0)
+    weight_grad(0, ur, late, 1, True)
+    w_1 = swap(0, 1)
+    turn(dg, every)
+    weight_grad(1, xr, every, 0)
+    w_2 = swap(1, 0)
     arrive([w_0])
-    ring_step(0, 0)
+    ring_step(0, 0, 0)
     arrive([w_1])
-    ring_step(0, 1)
+    ring_step(0, 0, 1)
+    weight_grad(1, xr, every, 1)
+    w_3 = swap(1, 1)
+    turn(du, every)
+    weight_grad(2, xr, every, 0)
+    w_4 = swap(2, 0)
     arrive([w_2])
-    ring_step(0, 2)
+    ring_step(0, 1, 0)
+    arrive([w_3])
+    ring_step(0, 1, 1)
+    weight_grad(2, xr, every, 1)
+    w_5 = swap(2, 1)
+    arrive([w_4])
+    ring_step(0, 2, 0)
+    arrive([w_5])
+    ring_step(0, 2, 1)
     arrive(r_c)
-    r_b = give_back("B")
     zsend[2] = product(ptc, 2 * tokn, "C", sides[0]).astype(BF16)
     z2 = send(zsend.at[2], zrecv.at[2], zup)
     zsend[3] = product(ptc, 2 * tokn, "C", sides[1]).astype(BF16)
     z3 = send(zsend.at[3], zrecv.at[3], zdown)
-    ring_step(1, 0)
-    ring_step(1, 1)
-    ring_step(1, 2)
+    r_b += give_back("B", (1, 3))
+    ring_step(1, 0, 0)
+    ring_step(1, 0, 1)
+    ring_step(1, 1, 0)
+    ring_step(1, 1, 1)
+    ring_step(1, 2, 0)
+    ring_step(1, 2, 1)
     arrive(r_b)
-    r_a = give_back("A")
     zsend[0] = near_part(0, 1).astype(BF16)
     z0 = send(zsend.at[0], zrecv.at[0], zup)
     zsend[1] = near_part(1, 0).astype(BF16)
     z1 = send(zsend.at[1], zrecv.at[1], zdown)
+    r_a = give_back("A")
+    ring_step(2, 0, 0)
+    ring_step(2, 0, 1)
     arrive([z2, z3])
     zsend[4] = (near_part(0, 0) + zrecv[2].astype(F32)).astype(BF16)
     z4 = send(zsend.at[4], zrecv.at[4], zup)
     zsend[5] = (near_part(1, 1) + zrecv[3].astype(F32)).astype(BF16)
     z5 = send(zsend.at[5], zrecv.at[5], zdown)
-    ring_step(2, 0)
-    ring_step(2, 1)
-    ring_step(2, 2)
-    for piece in range(3):
-        lo_step(piece)
+    ring_step(2, 1, 0)
+    ring_step(2, 1, 1)
+    ring_step(2, 2, 0)
+    ring_step(2, 2, 1)
+    lo_step(0)
     arrive(r_a)
+    for side in range(2):
+        own[:, sides[side]] = product(pta, 0, "A", sides[side]) + product(ptc, 3 * tokn, "C", sides[side])
+    lo_step(1)
+    finish(0)
+    lo_step(2)
+    finish(1)
+    finish(2)
     arrive([z0, z1, z4, z5])
     for side, parts in ((0, (1, 4)), (1, (0, 5))):
-        total = product(pta, 0, "A", sides[side]) + product(ptc, 3 * tokn, "C", sides[side])
+        total = own[:, sides[side]]
         for part in parts:
             total = total + zrecv[part].astype(F32)
         gt_out[:, sides[side]] = total.astype(BF16)
-    for piece in range(3):
-        finish(piece)
 
     already = [*x_a, *x_b, *x_c, *t_far, *c_0, *c_1, *c_far0]
     for copy in started:
@@ -451,7 +490,7 @@
     vmem = pl.BlockSpec(memory_space=pltpu.VMEM)
     anyw = pl.BlockSpec(memory_space=pl.ANY)
     v = pltpu.VMEM
-    copies = 81
+    copies = 102
     outs = pl.pallas_call(
         functools.partial(kernel, cap),
         out_shape=[
@@ -477,11 +516,11 @@
             v((nrows, hsize), BF16), v((nrows, hsize), BF16), v((nrows, hsize), BF16),
             v((nrows, feat), BF16),
             v((hsize, nrows), BF16),
-            v((NC, 3, NY, 2, NZL, hh, ds), BF16),
-            v((3, NY, 2, NZL, hh, ds), BF16),
-            v((NY - 1, 3, 2, NZL, hh, ds), BF16),
+            v((NC, 3, NZL, NY, 2, hh, ds), BF16),
+            v((3, NZL, NY, 2, hh, ds), BF16),
+            v((NY - 1, 3, NZL, 2, hh, ds), BF16),
             v((3, 2, hh, ds), BF16),
-            v((3, 2, hh, ds), F32),
+            v((tokn, feat), F32),
             v((6, tokn, feat // 2), BF16), v((6, tokn, feat // 2), BF16),
             pltpu.SemaphoreType.DMA((copies,)),
             pltpu.SemaphoreType.DMA((copies,)),

time: 167 us -> 168 us (level)
  no operation moved by 1% of the time
where the time goes in v5:
time: 168 us; the launch traced here: 167 us
  Pallas kernels  167 us (99%)
    pallas_call x1, Pallas kernels, on_device(): pl.pallas_call(functools.partial(kernel, cap), out_shape=[jax.ShapeDtypeS...  164 us

profile of v5, /device:TPU:1, one launch (start us, length us, event | category | flops | bytes accessed | tf_op | source)
XLA Modules:
  0.0 167.4 jit_solution(9868855704322963566)
XLA Ops:
  0.6 164.5 %shard_map.102 = (bf16[128,2048]{1,0:T(8,128)(2,1)}, f32[128,768]{1,0:T(8,128)}, f32[128,768]{1,0:T(8,128)}, f32[768,128]{1,0:T(8,128)}) custom-call(bf16[128,2048]{1,0:T(8,128)(2,1)} %tok.1, bf16[128,2048]{1,0:T(8,128)(2,1)} %cot.1, s32[4,128]{1,0:T(4,128)} %bitcast.11, s32[4,128]{1,0:T(4,128)} %bitcast.12, bf16[2048,768]{1,0:T(8,128)(2,1)} %bitcast.8, ...), custom_call_target="tpu_custom_call" | custom-call | tf_op jit(solution)/shard_map/pallas_call | solution.py:494
  165.1 2.3 %shard_map.103 = (bf16[128,2048]{1,0:T(8,128)(2,1)}, f32[128,768]{1,0:T(8,128)}, f32[128,768]{1,0:T(8,128)}, f32[768,128]{1,0:T(8,128)}) custom-call(bf16[128,2048]{1,0:T(8,128)(2,1)} %get-tuple-element.12.refs_0_, f32[128,768]{1,0:T(8,128)} %get-tuple-element.13.refs_1_, f32[128,768]{1,0:T(8,128)} %get-tuple-element.14.refs_2_, ...), custom_call_target="tpu_custom_call" | custom-call | tf_op jit(solution)/shard_map/pallas_call | solution.py:470

commit v6 on v5

--- a/solution.py
+++ b/solution.py
@@ -114,6 +114,8 @@
             send(buf.at[rws(fh, fh), cols], buf.at[rws(2 * tokn + fh, fh), cols], zdown),
         ]
 
+    c_0 = cot_near(0)
+
     earlier = (
         lax.broadcasted_iota(jnp.int32, (tokn, tokn), 0)
         < lax.broadcasted_iota(jnp.int32, (tokn, tokn), 1)
@@ -170,9 +172,12 @@
         for copy in copies:
             copy.wait_recv()
 
+    left_already = []
+
     def gone(copies):
         for copy in copies:
             copy.wait_send()
+        left_already.extend(copies)
 
     def front_x(chunk):
         n = 4 * rows[chunk]
@@ -254,31 +259,26 @@
 
     arrive([t_down, t_up])
     t_far = far(zt, whole)
+    c_1 = cot_near(1)
     select("B", pxb, zt, 0, 2 * tokn, sx, xr)
     x_b = spread("B", sx, xr)
     arrive(u_a)
     front_u("A")
-    gone(t_far)
-    c_0 = cot_near(0)
-    arrive(t_far)
-    select("C", pxc, zt, 0, 4 * tokn, sx, xr)
-    x_c = spread("C", sx, xr)
+    arrive(c_0)
+    c_far0 = far(zc, sides[0])
+    u_b = spread_cot("B", pub, 0, 2 * tokn, 0)
     gone(x_a)
     back_rows("A")
     arrive(x_b)
     front_x("B")
-    gone(c_0)
-    c_1 = cot_near(1)
-    arrive(c_0)
-    u_b = spread_cot("B", pub, 0, 2 * tokn, 0)
+    arrive(t_far)
+    select("C", pxc, zt, 0, 4 * tokn, sx, xr)
+    x_c = spread("C", sx, xr)
+    arrive(c_1)
+    c_far1 = far(zc, sides[1])
+    u_b += spread_cot("B", pub, 0, 2 * tokn, 1)
     arrive(x_c)
     front_x("C")
-    gone(c_1)
-    c_far0 = far(zc, sides[0])
-    arrive(c_1)
-    u_b += spread_cot("B", pub, 0, 2 * tokn, 1)
-    gone(c_far0)
-    c_far1 = far(zc, sides[1])
     arrive(c_far0)
     u_c = spread_cot("C", puc, 0, 4 * tokn, 0)
     arrive(u_b)
@@ -447,9 +447,8 @@
             total = total + zrecv[part].astype(F32)
         gt_out[:, sides[side]] = total.astype(BF16)
 
-    already = [*x_a, *x_b, *x_c, *t_far, *c_0, *c_1, *c_far0]
     for copy in started:
-        if not any(copy is one for one in already):
+        if not any(copy is one for one in left_already):
             copy.wait_send()
 
 

time: 168 us -> 164 us (0.976)
  Pallas kernels: 167 us -> 164 us
    pallas_call x1, Pallas kernels: 164 us -> 161 us  [on_device(): pl.pallas_call(functools.partial(kernel, cap), out_shape=[jax.ShapeDtypeS...]
where the time goes in v6:
time: 164 us
  Pallas kernels  164 us (100%)
    pallas_call x1, Pallas kernels, on_device(): pl.pallas_call(functools.partial(kernel, cap), out_shape=[jax.ShapeDtypeS...  161 us

profile of v6, /device:TPU:1, one launch (start us, length us, event | category | flops | bytes accessed | tf_op | source)
XLA Modules:
  0.0 164.3 jit_solution(8952840197562540383)
XLA Ops:
  0.6 161.4 %shard_map.102 = (bf16[128,2048]{1,0:T(8,128)(2,1)}, f32[128,768]{1,0:T(8,128)}, f32[128,768]{1,0:T(8,128)}, f32[768,128]{1,0:T(8,128)}) custom-call(bf16[128,2048]{1,0:T(8,128)(2,1)} %tok.1, bf16[128,2048]{1,0:T(8,128)(2,1)} %cot.1, s32[4,128]{1,0:T(4,128)} %bitcast.11, s32[4,128]{1,0:T(4,128)} %bitcast.12, bf16[2048,768]{1,0:T(8,128)(2,1)} %bitcast.8, ...), custom_call_target="tpu_custom_call" | custom-call | tf_op jit(solution)/shard_map/pallas_call | solution.py:493
  162.0 2.3 %shard_map.103 = (bf16[128,2048]{1,0:T(8,128)(2,1)}, f32[128,768]{1,0:T(8,128)}, f32[128,768]{1,0:T(8,128)}, f32[768,128]{1,0:T(8,128)}) custom-call(bf16[128,2048]{1,0:T(8,128)(2,1)} %get-tuple-element.12.refs_0_, f32[128,768]{1,0:T(8,128)} %get-tuple-element.13.refs_1_, f32[128,768]{1,0:T(8,128)} %get-tuple-element.14.refs_2_, ...), custom_call_target="tpu_custom_call" | custom-call | tf_op jit(solution)/shard_map/pallas_call | solution.py:469

commit v7 on v6

--- a/solution.py
+++ b/solution.py
@@ -57,7 +57,15 @@
     def at_dp(dzl, dy, dc):
         return ((((zl + dzl) % NZL) * NY + (y + dy) % NY) * NC + (core + dc) % NC, ex)
 
-    zup, zdown = at_ex(0, 1), at_ex(0, 3)
+    turned = 1 - 2 * zl
+
+    def at_z(dz, dzl):
+        return (
+            (((zl + dzl) % NZL) * NY + y) * NC + core,
+            x * NZ + (z + NZ + dz) % NZ,
+        )
+
+    znext, zprev, zside = at_z(turned, 0), at_z(-turned, 0), at_z(-turned, 1)
     yup, ydown = at_dp(0, 1, 0), at_dp(0, 3, 0)
     other, lopeer = at_dp(0, 0, 1), at_dp(1, 0, 0)
 
@@ -69,7 +77,7 @@
     for load in loads:
         load.start()
 
-    peers = [zup, zdown, at_ex(1, 0), at_ex(2, 0), at_ex(3, 0), yup, ydown, other, lopeer]
+    peers = [znext, zprev, zside, at_ex(1, 0), at_ex(2, 0), at_ex(3, 0), yup, ydown, other, lopeer]
     barrier = pltpu.get_barrier_semaphore()
     for peer in peers:
         pl.semaphore_signal(barrier, inc=1, device_id=peer, device_id_type=MESH)
@@ -96,23 +104,20 @@
         codes = codes + jnp.where(number == ids[k : k + 1, :], wts[k : k + 1, :].astype(F32), 0.0)
     gcode[...] = codes
 
-    g_down = send(gcode, gz.at[0], zdown)
-    g_up = send(gcode, gz.at[1], zup)
-    t_down = send(tok, zt.at[rws(0, tokn)], zdown)
-    t_up = send(tok, zt.at[rws(tokn, tokn)], zup)
+    g_side = send(gcode, gz.at[0], zside)
+    g_next = send(gcode, gz.at[1], znext)
+    t_side = send(tok, zt.at[rws(0, tokn)], zside)
+    t_next = send(tok, zt.at[rws(tokn, tokn)], znext)
 
     def cot_near(side):
         cols = pl.ds(side * half, half)
         return [
-            send(cot.at[:, cols], zc.at[rws(0, tokn), cols], zdown),
-            send(cot.at[:, cols], zc.at[rws(tokn, tokn), cols], zup),
+            send(cot.at[:, cols], zc.at[rws(0, tokn), cols], zside),
+            send(cot.at[:, cols], zc.at[rws(tokn, tokn), cols], znext),
         ]
 
     def far(buf, cols):
-        return [
-            send(buf.at[rws(tokn, fh), cols], buf.at[rws(2 * tokn, fh), cols], zup),
-            send(buf.at[rws(fh, fh), cols], buf.at[rws(2 * tokn + fh, fh), cols], zdown),
-        ]
+        return [send(buf.at[rws(0, tokn), cols], buf.at[rws(2 * tokn, tokn), cols], znext)]
 
     c_0 = cot_near(0)
 
@@ -238,8 +243,8 @@
     zc[rws(3 * tokn, tokn), :] = cot[...]
     place_extra(0, gcode, 0, 3)
 
-    arrive([g_down, g_up])
-    g_far = send(gz.at[1], gz.at[2], zup)
+    arrive([g_side, g_next])
+    g_far = send(gz.at[0], gz.at[2], znext)
     rank(1, gz[0])
     rank(2, gz[1])
     place(1, gz.at[0], 2 * main, 0, pxb, pub, pl.ds(0, tokn), 0, main)
@@ -257,9 +262,10 @@
     arrive(x_a)
     front_x("A")
 
-    arrive([t_down, t_up])
+    arrive([t_side])
     t_far = far(zt, whole)
     c_1 = cot_near(1)
+    arrive([t_next])
     select("B", pxb, zt, 0, 2 * tokn, sx, xr)
     x_b = spread("B", sx, xr)
     arrive(u_a)
@@ -404,9 +410,9 @@
     ring_step(0, 2, 1)
     arrive(r_c)
     zsend[2] = product(ptc, 2 * tokn, "C", sides[0]).astype(BF16)
-    z2 = send(zsend.at[2], zrecv.at[2], zup)
+    z2 = send(zsend.at[2], zrecv.at[2], zprev)
     zsend[3] = product(ptc, 2 * tokn, "C", sides[1]).astype(BF16)
-    z3 = send(zsend.at[3], zrecv.at[3], zdown)
+    z3 = send(zsend.at[3], zrecv.at[3], zprev)
     r_b += give_back("B", (1, 3))
     ring_step(1, 0, 0)
     ring_step(1, 0, 1)
@@ -415,18 +421,18 @@
     ring_step(1, 2, 0)
     ring_step(1, 2, 1)
     arrive(r_b)
-    zsend[0] = near_part(0, 1).astype(BF16)
-    z0 = send(zsend.at[0], zrecv.at[0], zup)
-    zsend[1] = near_part(1, 0).astype(BF16)
-    z1 = send(zsend.at[1], zrecv.at[1], zdown)
+    zsend[0] = near_part(1, 0).astype(BF16)
+    z0 = send(zsend.at[0], zrecv.at[0], zprev)
+    zsend[1] = near_part(1, 1).astype(BF16)
+    z1 = send(zsend.at[1], zrecv.at[1], zprev)
     r_a = give_back("A")
     ring_step(2, 0, 0)
     ring_step(2, 0, 1)
     arrive([z2, z3])
     zsend[4] = (near_part(0, 0) + zrecv[2].astype(F32)).astype(BF16)
-    z4 = send(zsend.at[4], zrecv.at[4], zup)
-    zsend[5] = (near_part(1, 1) + zrecv[3].astype(F32)).astype(BF16)
-    z5 = send(zsend.at[5], zrecv.at[5], zdown)
+    z4 = send(zsend.at[4], zrecv.at[4], zside)
+    zsend[5] = (near_part(0, 1) + zrecv[3].astype(F32)).astype(BF16)
+    z5 = send(zsend.at[5], zrecv.at[5], zside)
     ring_step(2, 1, 0)
     ring_step(2, 1, 1)
     ring_step(2, 2, 0)
@@ -441,7 +447,7 @@
     finish(1)
     finish(2)
     arrive([z0, z1, z4, z5])
-    for side, parts in ((0, (1, 4)), (1, (0, 5))):
+    for side, parts in ((0, (0, 4)), (1, (1, 5))):
         total = own[:, sides[side]]
         for part in parts:
             total = total + zrecv[part].astype(F32)
@@ -489,7 +495,7 @@
     vmem = pl.BlockSpec(memory_space=pltpu.VMEM)
     anyw = pl.BlockSpec(memory_space=pl.ANY)
     v = pltpu.VMEM
-    copies = 102
+    copies = 99
     outs = pl.pallas_call(
         functools.partial(kernel, cap),
         out_shape=[

time: 164 us -> 160 us (0.976); the launches traced: 164 us -> 159 us
  Pallas kernels: 164 us -> 158 us
    pallas_call x1, Pallas kernels: 161 us -> 156 us  [on_device(): pl.pallas_call(functools.partial(kernel, cap), out_shape=[jax.ShapeDtypeS...]
where the time goes in v7:
time: 160 us; the launch traced here: 159 us
  Pallas kernels  158 us (99%)
    pallas_call x1, Pallas kernels, on_device(): pl.pallas_call(functools.partial(kernel, cap), out_shape=[jax.ShapeDtypeS...  156 us

profile of v7, /device:TPU:1, one launch (start us, length us, event | category | flops | bytes accessed | tf_op | source)
XLA Modules:
  0.0 158.6 jit_solution(11911749504036107884)
XLA Ops:
  0.6 155.7 %shard_map.102 = (bf16[128,2048]{1,0:T(8,128)(2,1)}, f32[128,768]{1,0:T(8,128)}, f32[128,768]{1,0:T(8,128)}, f32[768,128]{1,0:T(8,128)}) custom-call(bf16[128,2048]{1,0:T(8,128)(2,1)} %tok.1, bf16[128,2048]{1,0:T(8,128)(2,1)} %cot.1, s32[4,128]{1,0:T(4,128)} %bitcast.11, s32[4,128]{1,0:T(4,128)} %bitcast.12, bf16[2048,768]{1,0:T(8,128)(2,1)} %bitcast.8, ...), custom_call_target="tpu_custom_call" | custom-call | tf_op jit(solution)/shard_map/pallas_call | solution.py:499
  156.3 2.3 %shard_map.103 = (bf16[128,2048]{1,0:T(8,128)(2,1)}, f32[128,768]{1,0:T(8,128)}, f32[128,768]{1,0:T(8,128)}, f32[768,128]{1,0:T(8,128)}) custom-call(bf16[128,2048]{1,0:T(8,128)(2,1)} %get-tuple-element.12.refs_0_, f32[128,768]{1,0:T(8,128)} %get-tuple-element.13.refs_1_, f32[128,768]{1,0:T(8,128)} %get-tuple-element.14.refs_2_, ...), custom_call_target="tpu_custom_call" | custom-call | tf_op jit(solution)/shard_map/pallas_call | solution.py:475

commit v8 on v7

--- a/solution.py
+++ b/solution.py
@@ -223,12 +223,12 @@
             rr[rws(off[chunk], n), cols] = got[:n]
             sx[rws(soff[chunk], 3 * n), cols] = got[n:]
 
-    def give_back(chunk, ways=(2, 1, 3)):
+    def give_back(chunk, ways=(2, 1, 3), cols=whole):
         n = rows[chunk]
         return [
             send(
-                sx.at[rws(soff[chunk] + (k - 1) * n, n)], rr.at[rws(off[chunk] + k * n, n)],
-                at_ex(NX - k, 0),
+                sx.at[rws(soff[chunk] + (k - 1) * n, n), cols],
+                rr.at[rws(off[chunk] + k * n, n), cols], at_ex(NX - k, 0),
             )
             for k in ways
         ]
@@ -377,7 +377,7 @@
     weight_grad(0, ur, early, 1)
     turn(hid, late)
     arrive(u_c)
-    r_b = give_back("B", (2,))
+    r_b = give_back("B", (2,), sides[0])
     front_u("C")
     gone(x_c)
     back_rows("C")
@@ -387,10 +387,10 @@
     weight_grad(0, ur, late, 1, True)
     w_1 = swap(0, 1)
     turn(dg, every)
+    arrive([w_0])
+    ring_step(0, 0, 0)
     weight_grad(1, xr, every, 0)
     w_2 = swap(1, 0)
-    arrive([w_0])
-    ring_step(0, 0, 0)
     arrive([w_1])
     ring_step(0, 0, 1)
     weight_grad(1, xr, every, 1)
@@ -413,7 +413,7 @@
     z2 = send(zsend.at[2], zrecv.at[2], zprev)
     zsend[3] = product(ptc, 2 * tokn, "C", sides[1]).astype(BF16)
     z3 = send(zsend.at[3], zrecv.at[3], zprev)
-    r_b += give_back("B", (1, 3))
+    r_b += give_back("B", (2,), sides[1]) + give_back("B", (1, 3))
     ring_step(1, 0, 0)
     ring_step(1, 0, 1)
     ring_step(1, 1, 0)
@@ -495,7 +495,7 @@
     vmem = pl.BlockSpec(memory_space=pltpu.VMEM)
     anyw = pl.BlockSpec(memory_space=pl.ANY)
     v = pltpu.VMEM
-    copies = 99
+    copies = 100
     outs = pl.pallas_call(
         functools.partial(kernel, cap),
         out_shape=[

time: 160 us -> 161 us (level)
  Pallas kernels: 158 us -> 160 us
    pallas_call x1, Pallas kernels: 156 us -> 158 us  [on_device(): pl.pallas_call(functools.partial(kernel, cap), out_shape=[jax.ShapeDtypeS...]
where the time goes in v8:
time: 161 us
  Pallas kernels  160 us (99%)
    pallas_call x1, Pallas kernels, on_device(): pl.pallas_call(functools.partial(kernel, cap), out_shape=[jax.ShapeDtypeS...  158 us

profile of v8, /device:TPU:1, one launch (start us, length us, event | category | flops | bytes accessed | tf_op | source)
XLA Modules:
  0.0 161.1 jit_solution(3393167905108456274)
XLA Ops:
  0.6 158.2 %shard_map.102 = (bf16[128,2048]{1,0:T(8,128)(2,1)}, f32[128,768]{1,0:T(8,128)}, f32[128,768]{1,0:T(8,128)}, f32[768,128]{1,0:T(8,128)}) custom-call(bf16[128,2048]{1,0:T(8,128)(2,1)} %tok.1, bf16[128,2048]{1,0:T(8,128)(2,1)} %cot.1, s32[4,128]{1,0:T(4,128)} %bitcast.11, s32[4,128]{1,0:T(4,128)} %bitcast.12, bf16[2048,768]{1,0:T(8,128)(2,1)} %bitcast.8, ...), custom_call_target="tpu_custom_call" | custom-call | tf_op jit(solution)/shard_map/pallas_call | solution.py:499
  158.8 2.3 %shard_map.103 = (bf16[128,2048]{1,0:T(8,128)(2,1)}, f32[128,768]{1,0:T(8,128)}, f32[128,768]{1,0:T(8,128)}, f32[768,128]{1,0:T(8,128)}) custom-call(bf16[128,2048]{1,0:T(8,128)(2,1)} %get-tuple-element.12.refs_0_, f32[128,768]{1,0:T(8,128)} %get-tuple-element.13.refs_1_, f32[128,768]{1,0:T(8,128)} %get-tuple-element.14.refs_2_, ...), custom_call_target="tpu_custom_call" | custom-call | tf_op jit(solution)/shard_map/pallas_call | solution.py:475
